TPU v7x, 128 devices: a whole 4x4x4 slice. The times are simulated.
128 devices in a mesh: row: 4 (over x), col: 32 (over y, z, core).
Axes of the slice: x: 4, y: 4, z: 4, core: 2. Of those that a mesh axis runs over, the one named last changes fastest.
Arguments:
- trailing: float32 [15360, 15360], P('row', 'col'), as said below
- first_panel: float32 [15360, 512], P(('row', 'col')), may hold values from -0.046875 to 0.046875
- first_gram: float32 [512, 512], replicated, as said below
- second_panel: float32 [15360, 512], P(('row', 'col')), may hold values from -0.046875 to 0.046875
- second_lead: float32 [512, 512], replicated, may hold values from -0.046875 to 0.046875
- second_gram: float32 [512, 512], replicated, as said below
- tile_owner: int32 [24576, 1], P(('row', 'col')), may hold values from 0 to 127; in each aligned block of 192 rows (0 to 191, 192 to 383, ...) at most 2 rows name the same one
- tile_rows: int32 [24576, 128], P(('row', 'col')), may hold values from -1 to 479, as said below
- tile_block: int32 [24576], P(('row', 'col')), may hold values from 0 to 3
- tile_count: int32 [128], P(('row', 'col')), may hold values from 144 to 192
Outputs:
- first_column: float32 [15360, 512], P('col')
- first_corner: float32 [512, 512], P('col')
- second_upper: float32 [512, 512], P('col')
- second_column: float32 [15360, 512], P('col')
- second_corner: float32 [512, 512], P('col')
- child_tiles: bfloat16 [32768, 128, 128], P(('row', 'col'))
Inputs may be any that keep to these rules, and one draw needn't show every extreme that they name: trailing is exactly symmetric. first_gram is exactly symmetric. second_gram is exactly symmetric. `tile_owner`: among the tiles of one device no owner is named more than 2 times. `tile_rows`: in each tile the live indices come first and the rest are -1; a live index points into the sender's own block of 15360 / (devices along col) rows.
All inputs are finite; a program needn't handle non-finite values.
Results may differ from a plain program's by a relative error of at most 0.012.
Values may be sent and summed in bfloat16 or wider, within the bound.
No kernel may reach another device: no remote copies, remote signals or barrier semaphores. Data moves between devices by JAX's collectives and lax.ppermute only.
A program may use at most 192 MiB of HBM per device.

v0:
```python
import jax
import jax.numpy as jnp
from jax import lax
from jax.sharding import PartitionSpec as P

P_SIZE = 512
TILE = 128
TILE_CAP = 2


def broadcast(value, axis, source):
    kept = jnp.where(lax.axis_index(axis) == source, value, 0).astype(value.dtype)
    return lax.psum(kept, axis)


def multiply(left, right):
    return jnp.dot(left, right, precision=lax.Precision.HIGHEST, preferred_element_type=jnp.float32)


def contract_rows(left, right):
    return lax.dot_general(
        left,
        right,
        (((0,), (0,)), ((), ())),
        precision=lax.Precision.HIGHEST,
        preferred_element_type=jnp.float32,
    )


def column_share(value):
    return lax.psum_scatter(
        value.astype(jnp.bfloat16), "col", scatter_dimension=0, tiled=True
    ).astype(jnp.float32)


def shards(
    trailing,
    first_panel,
    first_gram,
    second_panel,
    second_lead,
    second_gram,
    tile_owner,
    tile_rows,
    tile_block,
    tile_count,
):
    row_count = lax.axis_size("row")
    col_count = lax.axis_size("col")
    col_index = lax.axis_index("col")
    local_rows = trailing.shape[1]
    stride = col_count // row_count
    source_row = col_index // stride
    offset = col_index % stride * local_rows
    gram_rows = P_SIZE // col_count
    gram_start = col_index * gram_rows

    def gram_slice(value):
        return lax.dynamic_slice_in_dim(value, gram_start, gram_rows, 0)

    def panel_terms(factor_block):
        gathered = lax.all_gather(factor_block, "col", axis=0, tiled=True)
        partial_value = contract_rows(trailing, gathered)
        own_rows = lax.dynamic_slice_in_dim(gathered, offset, local_rows, 0)
        shared = broadcast(own_rows.astype(jnp.bfloat16), "row", source_row).astype(own_rows.dtype)
        return (lax.psum(partial_value, "row"), shared)

    terms_one, shared_one = panel_terms(first_panel)
    first_column = -terms_one
    first_corner = gram_slice(first_gram) - column_share(contract_rows(shared_one, first_column))
    terms_two, shared_two = panel_terms(second_panel)
    second_column = -(terms_two + multiply(first_column, second_lead))
    second_upper = -(
        multiply(first_corner, second_lead) + column_share(contract_rows(first_column, shared_two))
    )
    lead_rows = gram_slice(second_lead)
    second_corner = gram_slice(second_gram) - column_share(
        contract_rows(lead_rows, second_upper) + contract_rows(shared_two, second_column)
    )
    band_rows = second_column.shape[0]
    block_count = P_SIZE // TILE
    tile_total = tile_rows.shape[0]
    group_size = 8
    band_low = second_column.astype(jnp.bfloat16)
    row_ids = jnp.arange(band_rows, dtype=jnp.int32)
    block_ids = jnp.arange(block_count, dtype=jnp.int32)

    def pick_group(operands):
        rows_group, blocks_group = operands
        selector = (
            (rows_group[:, :, None] == row_ids[None, None, :])
            .astype(jnp.bfloat16)
            .reshape(group_size * TILE, band_rows)
        )
        wide = jnp.dot(selector, band_low, preferred_element_type=jnp.float32).reshape(
            group_size, TILE, block_count, TILE
        )
        chooser = (blocks_group[:, None] == block_ids[None, :]).astype(jnp.float32)
        return jnp.einsum("gibj,gb->gij", wide, chooser).astype(jnp.bfloat16)

    tiles = lax.map(
        pick_group,
        (
            tile_rows.reshape(tile_total // group_size, group_size, TILE),
            tile_block.reshape(tile_total // group_size, group_size),
        ),
    )
    tiles = tiles.reshape(tile_total, TILE * TILE)
    owners = tile_owner[:, 0]
    order_ids = jnp.arange(tile_total, dtype=jnp.int32)
    live = order_ids < tile_count[0]
    earlier = (
        (owners[:, None] == owners[None, :])
        & live[None, :]
        & (order_ids[None, :] < order_ids[:, None])
    )
    slots = jnp.sum(earlier.astype(jnp.int32), axis=1)
    device_count = row_count * col_count
    dump = device_count * TILE_CAP
    target_slot = jnp.where(live, owners * TILE_CAP + slots, dump)
    placement_table = (target_slot[None, :] == jnp.arange(dump, dtype=jnp.int32)[:, None]).astype(
        jnp.bfloat16
    )
    outgoing = jnp.dot(placement_table, tiles, preferred_element_type=jnp.float32).astype(
        jnp.bfloat16
    )
    outgoing = outgoing.reshape(device_count, TILE_CAP, TILE, TILE)
    arrived = lax.all_to_all(outgoing, ("row", "col"), split_axis=0, concat_axis=0, tiled=True)
    child_tiles = arrived.reshape(device_count * TILE_CAP, TILE, TILE)
    return (first_column, first_corner, second_upper, second_column, second_corner, child_tiles)


def solution(mesh):
    in_specs = (
        P("row", "col"),
        P(("row", "col"), None),
        P(),
        P(("row", "col"), None),
        P(),
        P(),
        P(("row", "col"), None),
        P(("row", "col"), None),
        P(("row", "col")),
        P(("row", "col")),
    )
    out_specs = (
        P("col", None),
        P("col", None),
        P("col", None),
        P("col", None),
        P("col", None),
        P(("row", "col"), None, None),
    )
    return jax.shard_map(shards, mesh=mesh, in_specs=in_specs, out_specs=out_specs, check_vma=False)
```

profile of v0, /device:TPU:1, one launch (start us, length us, event | category | flops | bytes accessed | tf_op | source)
XLA Modules:
  0.0 645.4 jit_solution(3611201645771838497)
XLA Ops:
  8.7 57.2 %all-gather.5.cloned.1.call-done = f32[3840,512]{1,0:T(8,128)} async-done(((f32[120,512]{1,0:T(8,128)}), f32[3840,512]{1,0:T(8,128)}) %all-gather.5.cloned.1.call-update) | async-done | bytes 7864336 | tf_op jit(solution)/shard_map/all_gather | solution.py:62
  65.9 15.7 %fusion.31 = f32[480,512]{1,0:T(8,128)} fusion(f32[3840,480]{0,1:T(8,128)} %param.12, f32[3840,512]{1,0:T(8,128)} %all-gather.5.cloned.1.call-done), kind=kOutput, calls=%fused_computation.47 | convolution fusion | flops 11324620800 | bytes 16220160 | tf_op jit(solution)/shard_map/dot_general | solution.py:21
  81.6 37.9 %all-gather.3.cloned.1.call-done = f32[3840,512]{1,0:T(8,128)} async-done(((f32[120,512]{1,0:T(8,128)}), f32[3840,512]{1,0:T(8,128)}) %all-gather.3.cloned.1.call-update) | async-done | bytes 7864336 | tf_op jit(solution)/shard_map/all_gather | solution.py:62
  119.5 15.7 %fusion.30 = f32[480,512]{1,0:T(8,128)} fusion(f32[3840,480]{0,1:T(8,128)} %param.12, f32[3840,512]{1,0:T(8,128)} %all-gather.3.cloned.1.call-done), kind=kOutput, calls=%fused_computation.46 | convolution fusion | flops 11324620800 | bytes 16220160 | tf_op jit(solution)/shard_map/dot_general | solution.py:21
  136.2 54.9 %all-reduce.5.cloned.1.call-done = (f32[480,512]{1,0:T(8,128)}, f32[480,512]{1,0:T(8,128)}) async-done(((f32[480,512]{1,0:T(8,128)}, f32[480,512]{1,0:T(8,128)}), (f32[480,512]{1,0:T(8,128)}, f32[480,512]{1,0:T(8,128)})) %all-reduce.5.cloned.1.call-update) | async-done | bytes 1966096 | tf_op jit(solution)/shard_map/psum | solution.py:66
  191.1 1.3 neg.9
  192.4 3.3 fusion.29
  195.7 76.6 %while.11 = (s32[]{:T(128)}, bf16[24,8,128,128]{3,2,1,0:T(8,128)(2,1)}, s32[24,8,128]{2,1,0:T(8,128)}, bf16[480,512]{1,0:T(8,128)(2,1)S(1)}, s32[24,8]{1,0:T(8,128)S(1)}, /*index=5*/s32[]{:T(128)}) while((s32[]{:T(128)}, bf16[24,8,128,128]{3,2,1,0:T(8,128)(2,1)}, s32[24,8,128]{2,1,0:T(8,128)}, bf16[480,512]{1,0:T(8,128)(2,1)S(1)}, ...), condition=%wide.region_9.10_spmd.clone, body=%wide.region_8.9_spmd.clone.sunk | while | flops 504987680 | bytes 3911929 | solution.py:101
  197.3 0.9 fusion.63
  206.8 0.9 fusion.63
  213.2 0.9 fusion.63
  216.4 0.9 fusion.63
  232.4 0.9 fusion.63
  235.6 0.9 fusion.63
  257.9 0.9 fusion.63
  261.1 0.9 fusion.63
  272.3 10.9 %fusion.16 = bf16[32,8,128,128]{3,1,2,0:T(8,128)(2,1)} fusion(bf16[24,8,128,128]{3,2,1,0:T(8,128)(2,1)} %get-tuple-element.43, s32[192]{0:T(256)S(1)} %add_select_fusion), kind=kOutput, calls=%fused_computation.20 | convolution fusion | flops 1614856192 | bytes 14680832 | tf_op jit(solution)/shard_map/dot_general | solution.py:124
  283.3 9.2 %copy.23 = bf16[32,8,128,128]{3,2,1,0:T(8,128)(2,1)} copy(bf16[32,8,128,128]{3,1,2,0:T(8,128)(2,1)} %fusion.16) | data formatting | bytes 16777216
  292.5 8.6 %all-to-all-start = ((bf16[128,2,128,128]{3,2,1,0:T(8,128)(2,1)}), bf16[128,2,128,128]{3,2,1,0:T(8,128)(2,1)}, u32[]{:S(2)}, u32[]{:S(2)}) async-start(bf16[128,2,128,128]{3,2,1,0:T(8,128)(2,1)} %bitcast.76), calls=%async_computation.3 | async-start | bytes 16777216 | tf_op jit(solution)/shard_map/all_to_all | solution.py:128
  301.1 2.1 fusion.23
  303.3 2.1 fusion.22
  305.4 77.4 %all-reduce.7.cloned.1.call-done = (bf16[480,512]{1,0:T(8,128)(2,1)}, bf16[480,512]{1,0:T(8,128)(2,1)}) async-done(((bf16[480,512]{1,0:T(8,128)(2,1)}, bf16[480,512]{1,0:T(8,128)(2,1)}), (bf16[480,512]{1,0:T(8,128)(2,1)}, bf16[480,512]{1,0:T(8,128)(2,1)})) %all-reduce.7.cloned.1.call-update) | async-done | bytes 983056 | tf_op jit(solution)/shard_map/psum | solution.py:13
  382.8 3.0 convolution_convert_fusion.2
  385.9 2.9 convolution_convert_fusion.1
  389.1 76.7 %reduce-scatter.4.cloned.1.call-done = bf16[16,512]{1,0:T(8,128)(2,1)} async-done(((bf16[512,512]{1,0:T(8,128)(2,1)}), bf16[16,512]{1,0:T(8,128)(2,1)}) %reduce-scatter.4.cloned.1.call-update) | async-done | bytes 16400 | tf_op jit(solution)/shard_map/reduce_scatter | solution.py:31
  466.6 79.3 %reduce-scatter.6.cloned.1.call-done = bf16[16,512]{1,0:T(8,128)(2,1)} async-done(((bf16[512,512]{1,0:T(8,128)(2,1)}), bf16[16,512]{1,0:T(8,128)(2,1)}) %reduce-scatter.6.cloned.1.call-update) | async-done | bytes 16400 | tf_op jit(solution)/shard_map/reduce_scatter | solution.py:31
  545.9 1.3 fusion.21
  547.2 1.0 fusion.26
  548.3 1.9 fusion.20
  550.2 76.5 %reduce-scatter.8.cloned.1.call-done = bf16[16,512]{1,0:T(8,128)(2,1)} async-done(((bf16[512,512]{1,0:T(8,128)(2,1)}), bf16[16,512]{1,0:T(8,128)(2,1)}) %reduce-scatter.8.cloned.1.call-update) | async-done | bytes 16400 | tf_op jit(solution)/shard_map/reduce_scatter | solution.py:31
  626.7 1.4 convert_subtract_fusion
  628.1 10.5 %copy.57 = bf16[256,128,128]{2,1,0:T(8,128)(2,1)} copy(bf16[256,128,128]{2,1,0:T(8,128)(2,1)} %bitcast.3) | data formatting | bytes 16777216
  (173 shorter events, 72.1 us)
Async XLA Ops:
  7.2 185.2 %copy-start = (f32[512,512]{1,0:T(8,128)S(1)}, f32[512,512]{1,0:T(8,128)}, u32[]{:S(2)}) copy-start(f32[512,512]{1,0:T(8,128)} %param.16) | copy-start | bytes 3145732
  7.2 58.7 %all-gather.5.cloned.1.call-start = ((), (), s32[]{:S(2)}) async-start(), calls=%async_computation.6 | async-start | bytes 8110080 | tf_op jit(solution)/shard_map/all_gather | solution.py:62
  7.9 111.6 %all-gather.3.cloned.1.call-start = ((), (), s32[]{:S(2)}) async-start(), calls=%async_computation.4 | async-start | bytes 8110080 | tf_op jit(solution)/shard_map/all_gather | solution.py:62
  8.7 182.4 %all-reduce.5.cloned.1.call-start = ((), (), s32[]{:S(2)}) async-start(), calls=%async_computation.9 | async-start | bytes 3932160 | tf_op jit(solution)/shard_map/psum | solution.py:66
  81.6 54.3 %copy-start.7 = (s32[192]{0:T(256)S(1)}, s32[192]{0:T(256)}, u32[]{:S(2)}) copy-start(s32[192]{0:T(256)} %param.20) | copy-start | bytes 2308
  81.6 54.4 %copy-start.6 = (s32[192,1]{0,1:T(1,128)S(1)}, s32[192,1]{0,1:T(1,128)}, u32[]{:S(2)}) copy-start(s32[192,1]{0,1:T(1,128)} %param.18) | copy-start | bytes 2308
  192.3 193.5 %copy-start.1 = (f32[480,512]{1,0:T(8,128)}, f32[480,512]{1,0:T(8,128)S(1)}, u32[]{:S(2)}) copy-start(f32[480,512]{1,0:T(8,128)S(1)} %neg.9) | copy-start | bytes 2949124
  195.7 352.6 %copy-start.2 = (f32[480,512]{1,0:T(8,128)}, f32[480,512]{1,0:T(8,128)S(1)}, u32[]{:S(2)}) copy-start(f32[480,512]{1,0:T(8,128)S(1)} %get-tuple-element.131) | copy-start | bytes 2949124
  292.5 335.6 %all-to-all-start = ((bf16[128,2,128,128]{3,2,1,0:T(8,128)(2,1)}), bf16[128,2,128,128]{3,2,1,0:T(8,128)(2,1)}, u32[]{:S(2)}, u32[]{:S(2)}) async-start(bf16[128,2,128,128]{3,2,1,0:T(8,128)(2,1)} %bitcast.76), calls=%async_computation.3 | async-start | bytes 16777216 | tf_op jit(solution)/shard_map/all_to_all | solution.py:128
  301.1 81.8 %all-reduce.7.cloned.1.call-start = ((), (), s32[]{:S(2)}) async-start(), calls=%async_computation.10 | async-start | bytes 1966080 | tf_op jit(solution)/shard_map/psum | solution.py:13
  305.4 160.4 %reduce-scatter.4.cloned.1.call-start = ((), (), s32[]{:S(2)}) async-start(), calls=%async_computation.5 | async-start | bytes 540672 | tf_op jit(solution)/shard_map/reduce_scatter | solution.py:31
  382.8 165.4 %copy-start.3 = (bf16[480,512]{1,0:T(8,128)(2,1)S(1)}, bf16[480,512]{1,0:T(8,128)(2,1)}, u32[]{:S(2)}) copy-start(bf16[480,512]{1,0:T(8,128)(2,1)} %get-tuple-element.70) | copy-start | bytes 1474564
  385.8 160.0 %reduce-scatter.6.cloned.1.call-start = ((), (), s32[]{:S(2)}) async-start(), calls=%async_computation.7 | async-start | bytes 540672 | tf_op jit(solution)/shard_map/reduce_scatter | solution.py:31
  388.8 237.9 %reduce-scatter.8.cloned.1.call-start = ((), (), s32[]{:S(2)}) async-start(), calls=%async_computation.8 | async-start | bytes 540672 | tf_op jit(solution)/shard_map/reduce_scatter | solution.py:31
  466.6 172.0 %copy-start.5 = (f32[16,512]{1,0:T(8,128)}, f32[16,512]{1,0:T(8,128)S(1)}, u32[]{:S(2)}) copy-start(f32[16,512]{1,0:T(8,128)S(1)} %convert_subtract_fusion.1) | copy-start | bytes 98308
  547.2 91.4 %copy-start.4 = (f32[16,512]{1,0:T(8,128)}, f32[16,512]{1,0:T(8,128)S(1)}, u32[]{:S(2)}) copy-start(f32[16,512]{1,0:T(8,128)S(1)} %fusion.21) | copy-start | bytes 98308
Sparse Core Ops, SparseCore 0:
  10.3 55.5 all-gather.4
  68.1 51.3 all-gather.2
  135.3 55.6 all-reduce.4
  305.5 77.2 all-reduce.6
  387.1 78.6 reduce-scatter.3
  469.5 76.3 reduce-scatter.5
  550.3 76.3 reduce-scatter.7
where the time goes:
time: 648 us; the launch traced here: 645 us
  waiting for transfers between devices  461 us (71%)
  matrix products  95.6 us (15%)
  local copies, waits for them, and re-layouts  36.5 us (6%)
  other arithmetic  27.6 us (4%)
  between operations  14.9 us (2%)
  starting transfers between devices  9.09 us (1%)
    reduce_scatter x3, waiting for transfers between devices, column_share(): lax.psum_scatter(value.astype(jnp.bfloat16), 'col', scatter_dimension=0,...  233 us
    all_gather x2, waiting for transfers between devices, panel_terms(): gathered = lax.all_gather(factor_block, 'col', axis=0, tiled=True)  95.1 us
    psum x1, waiting for transfers between devices, broadcast(): return lax.psum(kept, axis)  77.4 us
    psum x1, waiting for transfers between devices, panel_terms(): return (lax.psum(partial_value, 'row'), shared)  54.9 us
    dot_general x6, matrix products, contract_rows(): lax.dot_general(left, right, (((0,), (0,)), ((), ())), precision=lax.Prec...  40.2 us
    dot_general x24, matrix products, pick_group(): return jnp.einsum('gibj,gb->gij', wide, chooser).astype(jnp.bfloat16)  21.5 us
    unnamed x18, local copies, waits for them, and re-layouts  19.8 us
    dot_general x24, matrix products, pick_group(): jnp.dot(selector, band_low, preferred_element_type=jnp.float32)  18.3 us
  transfers between devices with their start and end apart: 8, of which 7 were waited for; matrix products, arithmetic and copies ran while one was open for 5% of the time, Pallas kernels for 0%

commit v1 on v0

v1 whole, which is shorter than its diff:
```python
import functools

import jax
import jax.numpy as jnp
from jax import lax
from jax.experimental import pallas as pl
from jax.experimental.pallas import tpu as pltpu
from jax.sharding import PartitionSpec as P

P_SIZE = 512
TILE = 128
TILE_CAP = 2
CODE = 512


def precise(left, right):
    return jnp.dot(left, right, precision=lax.Precision.HIGHEST, preferred_element_type=jnp.float32)


def contract_rows(left, right):
    return lax.dot_general(
        left, right, (((0,), (0,)), ((), ())), preferred_element_type=jnp.float32
    )


def shift_rows(value, step):
    size = lax.axis_size("row")
    return lax.ppermute(value, "row", [(i, (i + step) % size) for i in range(size)])


def spread_rows(block):
    size = lax.axis_size("row")
    row = lax.axis_index("row")
    out = jnp.zeros((size,) + block.shape, block.dtype)
    out = lax.dynamic_update_index_in_dim(out, block, row, 0)
    for step in range(1, size):
        out = lax.dynamic_update_index_in_dim(out, shift_rows(block, step), (row - step) % size, 0)
    return out


def sum_rows(parts):
    size = lax.axis_size("row")
    row = lax.axis_index("row")
    total = lax.dynamic_index_in_dim(parts, row, 0, keepdims=False).astype(jnp.float32)
    for step in range(1, size):
        there = lax.dynamic_index_in_dim(parts, (row + step) % size, 0, keepdims=False)
        total = total + shift_rows(there, step).astype(jnp.float32)
    return total


def tile_kernel(blocks_ref, index_ref, band_ref, out_ref):
    band = pl.program_id(0)
    band_rows = band_ref.shape[1]
    senders, slots = out_ref.shape[0], out_ref.shape[2]
    columns = index_ref[0].T
    places = lax.broadcasted_iota(jnp.int32, (TILE, band_rows), 1)
    for sender in range(senders):
        for slot in range(slots):
            k = sender * slots + slot
            pick = jnp.where(columns[:, k : k + 1] == places, 1.0, 0.0).astype(jnp.bfloat16)
            start = pl.multiple_of(blocks_ref[band, k] * TILE, TILE)
            out_ref[sender, 0, slot] = jnp.dot(
                pick, band_ref[0, :, pl.ds(start, TILE)], preferred_element_type=jnp.float32
            ).astype(jnp.bfloat16)


def build_tiles(blocks, index, bands, row_count):
    col_count, band_rows, width = bands.shape
    return pl.pallas_call(
        tile_kernel,
        grid_spec=pltpu.PrefetchScalarGridSpec(
            num_scalar_prefetch=1,
            grid=(col_count,),
            in_specs=[
                pl.BlockSpec((1, row_count * TILE_CAP, TILE), lambda b, _: (b, 0, 0)),
                pl.BlockSpec((1, band_rows, width), lambda b, _: (b, 0, 0)),
            ],
            out_specs=pl.BlockSpec(
                (row_count, 1, TILE_CAP, TILE, TILE), lambda b, _: (0, b, 0, 0, 0)
            ),
        ),
        out_shape=jax.ShapeDtypeStruct(
            (row_count, col_count, TILE_CAP, TILE, TILE), jnp.bfloat16
        ),
        compiler_params=pltpu.CompilerParams(vmem_limit_bytes=32 * 1024 * 1024),
        cost_estimate=pl.CostEstimate(
            flops=2 * 256 * TILE * TILE * band_rows, bytes_accessed=25_000_000, transcendentals=0
        ),
    )(blocks, index, bands)


def route_indices(tile_owner, tile_rows, tile_block, tile_count, device_count):
    tile_total = tile_rows.shape[0]
    owners = tile_owner[:, 0]
    order_ids = jnp.arange(tile_total, dtype=jnp.int32)
    live = order_ids < tile_count[0]
    earlier = (
        (owners[:, None] == owners[None, :])
        & live[None, :]
        & (order_ids[None, :] < order_ids[:, None])
    )
    slots = jnp.sum(earlier.astype(jnp.int32), axis=1)
    dump = device_count * TILE_CAP
    target = jnp.where(live, owners * TILE_CAP + slots, dump)
    table = (target[None, :] == jnp.arange(dump, dtype=jnp.int32)[:, None]).astype(jnp.float32)
    coded = jnp.where(tile_rows >= 0, tile_rows + 1 + CODE * tile_block[:, None], 0)
    placed = precise(table, coded.astype(jnp.float32))
    sent = placed.reshape(device_count, TILE_CAP, TILE)
    return lax.all_to_all(sent, ("row", "col"), split_axis=0, concat_axis=0, tiled=True)


def shards(
    trailing,
    first_panel,
    first_gram,
    second_panel,
    second_lead,
    second_gram,
    tile_owner,
    tile_rows,
    tile_block,
    tile_count,
):
    row_count = lax.axis_size("row")
    col_count = lax.axis_size("col")
    row_index = lax.axis_index("row")
    col_index = lax.axis_index("col")
    device_count = row_count * col_count
    part_rows = first_panel.shape[0]
    gram_rows = P_SIZE // col_count
    low = jnp.bfloat16

    panels = jnp.concatenate(
        [first_panel, second_panel - precise(first_panel, second_lead)], axis=1
    ).astype(low)
    gathered = lax.all_gather(panels, "col", axis=0, tiled=True)

    perm = []
    for there in range(device_count):
        row, col = divmod(there, col_count)
        perm.append((col * row_count + row, there))
    own = spread_rows(lax.ppermute(panels, ("row", "col"), perm)).reshape(-1, 2 * P_SIZE)

    coded = route_indices(tile_owner, tile_rows, tile_block, tile_count, device_count)
    coded = coded.astype(jnp.int32).reshape(row_count, col_count, TILE_CAP, TILE)
    coded = coded.transpose(1, 0, 2, 3).reshape(col_count, row_count * TILE_CAP, TILE)
    index = coded % CODE - 1
    blocks = coded[:, :, 0] // CODE

    product = -contract_rows(trailing.astype(low), gathered)
    mine = sum_rows(product.astype(low).reshape(row_count, part_rows, 2 * P_SIZE))
    columns = spread_rows(mine.astype(low)).reshape(-1, 2 * P_SIZE)
    first_column = columns[:, :P_SIZE].astype(jnp.float32)
    second_low = columns[:, P_SIZE:]
    second_column = second_low.astype(jnp.float32)

    bands = lax.all_gather(second_low, "col", axis=0, tiled=False)
    tiles = build_tiles(blocks, index, bands, row_count)
    child_tiles = tiles.reshape(device_count * TILE_CAP, TILE, TILE)

    width = P_SIZE // row_count
    start = row_index * width
    first_part = lax.dynamic_slice_in_dim(columns, start, width, 1)
    second_part = lax.dynamic_slice_in_dim(columns, P_SIZE + start, width, 1)
    against_first = contract_rows(own[:, :P_SIZE], jnp.concatenate([first_part, second_part], 1))
    against_second = contract_rows(own[:, P_SIZE:], second_part)
    sums = jnp.concatenate([against_first, against_second], axis=1).astype(low)
    sums = sums.reshape(col_count, gram_rows, 3 * width)
    sums = lax.all_to_all(sums, "col", split_axis=0, concat_axis=0, tiled=True)
    sums = jnp.sum(sums.astype(jnp.float32), axis=0)
    sums = spread_rows(sums).reshape(row_count, gram_rows, 3, width)
    sums = sums.transpose(2, 1, 0, 3).reshape(3, gram_rows, P_SIZE)

    gram_start = col_index * gram_rows
    gram_part = lax.dynamic_slice_in_dim(first_gram, gram_start, gram_rows, 0)
    lead_part = lax.dynamic_slice_in_dim(second_lead, gram_start, gram_rows, 1)
    first_corner = gram_part - sums[0]
    second_upper = -(precise(gram_part, second_lead) + sums[1])
    second_corner = (
        lax.dynamic_slice_in_dim(second_gram, gram_start, gram_rows, 0)
        + precise(precise(lead_part.T, first_gram), second_lead)
        - sums[2]
    )
    return (first_column, first_corner, second_upper, second_column, second_corner, child_tiles)


def solution(mesh):
    in_specs = (
        P("row", "col"),
        P(("row", "col"), None),
        P(),
        P(("row", "col"), None),
        P(),
        P(),
        P(("row", "col"), None),
        P(("row", "col"), None),
        P(("row", "col")),
        P(("row", "col")),
    )
    out_specs = (
        P("col", None),
        P("col", None),
        P("col", None),
        P("col", None),
        P("col", None),
        P(("row", "col"), None, None),
    )
    return jax.shard_map(shards, mesh=mesh, in_specs=in_specs, out_specs=out_specs, check_vma=False)
```

time: 648 us -> 223 us (0.34)
  waiting for transfers between devices: 461 us -> 124 us
  matrix products: 95.6 us -> 18.8 us
  local copies, waits for them, and re-layouts: 36.5 us -> 9.2 us
  Pallas kernels: 0 us -> 21.6 us
  other arithmetic: 27.6 us -> 6.53 us
  starting transfers between devices: 9.09 us -> 27.7 us
    reduce_scatter x3 -> x0, waiting for transfers between devices: 233 us -> none  [column_share(): lax.psum_scatter(value.astype(jnp.bfloat16), 'col', scatter_dimension=0,...]
    psum x2 -> x0, waiting for transfers between devices: 132 us -> none  [the longest x1 77.4 us: broadcast(): return lax.psum(kept, axis)]
    dot_general x57 -> x8, matrix products: 95.6 us -> 18.8 us  [the longest x3 12.1 us: contract_rows(): lax.dot_general(left, right, (((0,), (0,)), ((), ())), preferred_element_...]
    ppermute x0 -> x13, waiting for transfers between devices: none -> 30.5 us  [the longest x12 30.5 us: shift_rows(): lax.ppermute(value, 'row', [(i, (i + step) % size) for i in range(size)])]
    pallas_call x0 -> x1, Pallas kernels: none -> 21.6 us  [build_tiles(): pl.pallas_call(tile_kernel, grid_spec=pltpu.PrefetchScalarGridSpec(num_sc...]
    all_gather x2, waiting for transfers between devices: 95.1 us -> 74 us  [the longest x1 51.1 us: shards(): gathered = lax.all_gather(panels, 'col', axis=0, tiled=True)]
    all_to_all x1 -> x2, waiting for transfers between devices: 0.01 us -> 19.4 us  [the longest x1 10.4 us: shards(): sums = lax.all_to_all(sums, 'col', split_axis=0, concat_axis=0, tiled=True)]
    eq x48 -> x0, local copies, waits for them, and re-layouts: 16.7 us -> none  [the longest x24 16.5 us: pick_group(): rows_group[:, :, None] == row_ids[None, None, :]]
  transfers between devices with their start and end apart: 8 -> 17, of which waited for: 7 -> 11; matrix products, arithmetic and copies ran while one was open for 5% -> 10% of each run, Pallas kernels for 0% -> 0%
where the time goes in v1:
time: 223 us
  waiting for transfers between devices  124 us (56%)
  starting transfers between devices  27.7 us (12%)
  Pallas kernels  21.6 us (10%)
  matrix products  18.8 us (8%)
  between operations  15.1 us (7%)
  local copies, waits for them, and re-layouts  9.2 us (4%)
  other arithmetic  6.53 us (3%)
    all_gather x1, waiting for transfers between devices, shards(): gathered = lax.all_gather(panels, 'col', axis=0, tiled=True)  51.1 us
    ppermute x12, waiting for transfers between devices, shift_rows(): lax.ppermute(value, 'row', [(i, (i + step) % size) for i in range(size)])  30.5 us
    all_gather x1, waiting for transfers between devices, shards(): bands = lax.all_gather(second_low, 'col', axis=0, tiled=False)  22.9 us
    pallas_call x1, Pallas kernels, build_tiles(): pl.pallas_call(tile_kernel, grid_spec=pltpu.PrefetchScalarGridSpec(num_sc...  21.6 us
    dot_general x3, matrix products, contract_rows(): lax.dot_general(left, right, (((0,), (0,)), ((), ())), preferred_element_...  12.1 us
    all_to_all x1, waiting for transfers between devices, shards(): sums = lax.all_to_all(sums, 'col', split_axis=0, concat_axis=0, tiled=True)  10.4 us
    ppermute x12, starting transfers between devices, shift_rows(): lax.ppermute(value, 'row', [(i, (i + step) % size) for i in range(size)])  10.3 us
    all_to_all x1, waiting for transfers between devices, route_indices(): lax.all_to_all(sent, ('row', 'col'), split_axis=0, concat_axis=0, tiled=T...  9.03 us
  transfers between devices with their start and end apart: 17, of which 11 were waited for; matrix products, arithmetic and copies ran while one was open for 10% of the time, Pallas kernels for 0%

profile of v1, /device:TPU:1, one launch (start us, length us, event | category | flops | bytes accessed | tf_op | source)
XLA Modules:
  0.0 222.9 jit_solution(14354382954292495327)
XLA Ops:
  7.2 1.0 convert.15
  8.5 1.8 fusion.4
  11.1 4.5 %collective-permute-start.6 = (bf16[120,1024]{1,0:T(8,128)(2,1)}, bf16[120,1024]{1,0:T(8,128)(2,1)S(1)}, u32[]{:S(2)}, u32[]{:S(2)}) collective-permute-start(bf16[120,1024]{1,0:T(8,128)(2,1)} %pad_maximum_fusion.1), channel_id=1, source_target_pairs={{0,0},{4,1},{8,2},{12,3},{16,4},{20,5},{24,6},{28,7},{32,8},{36,9}... | collective-permute-start | bytes 737288 | tf_op jit(solution)/shard_map/ppermute | solution.py:142
  15.7 51.1 %all-gather.4.cloned.1.call-done = bf16[3840,1024]{1,0:T(8,128)(2,1)} async-done(((bf16[120,1024]{1,0:T(8,128)(2,1)}), bf16[3840,1024]{1,0:T(8,128)(2,1)}) %all-gather.4.cloned.1.call-update) | async-done | bytes 7864336 | tf_op jit(solution)/shard_map/all_gather | solution.py:136
  66.8 9.3 %negate_convert_fusion = bf16[1024,480]{0,1:T(8,128)(2,1)S(1)} fusion(bf16[3840,1024]{1,0:T(8,128)(2,1)} %all-gather.4.cloned.1.call-done, f32[3840,480]{0,1:T(8,128)} %param.10), kind=kOutput, calls=%fused_computation.2 | convolution fusion | flops 3777699840 | bytes 16220160 | tf_op jit(solution)/shard_map/dot_general | solution.py:21
  77.1 1.3 collective-permute-start
  78.3 1.5 collective-permute-start.2
  79.8 1.5 collective-permute-start.1
  82.2 1.2 collective-permute-start.8
  83.5 2.1 collective-permute-done
  86.3 5.6 %collective-permute-done.1 = bf16[120,1024]{1,0:T(8,128)(2,1)} collective-permute-done((bf16[120,1024]{1,0:T(8,128)(2,1)S(1)}, bf16[120,1024]{1,0:T(8,128)(2,1)}, u32[]{:S(2)}, u32[]{:S(2)}) %collective-permute-start.1) | collective-permute-done | bytes 245792 | tf_op jit(solution)/shard_map/ppermute | solution.py:28
  92.1 1.5 bitcast_dynamic-update-slice_fusion.7
  94.2 8.7 %collective-permute-done.7 = bf16[120,1024]{1,0:T(8,128)(2,1)S(1)} collective-permute-done((bf16[120,1024]{1,0:T(8,128)(2,1)S(1)}, bf16[120,1024]{1,0:T(8,128)(2,1)S(1)}, u32[]{:S(2)}, u32[]{:S(2)}) %collective-permute-start.7) | collective-permute-done | bytes 245792 | tf_op jit(solution)/shard_map/ppermute | solution.py:28
  104.0 4.7 %collective-permute-done.3 = bf16[120,1024]{1,0:T(8,128)(2,1)S(1)} collective-permute-done((bf16[120,1024]{1,0:T(8,128)(2,1)S(1)}, bf16[120,1024]{1,0:T(8,128)(2,1)S(1)}, u32[]{:S(2)}, u32[]{:S(2)}) %collective-permute-start.3) | collective-permute-done | bytes 245792 | tf_op jit(solution)/shard_map/ppermute | solution.py:28
  108.7 4.2 %collective-permute-done.4 = bf16[120,1024]{1,0:T(8,128)(2,1)S(1)} collective-permute-done((bf16[120,1024]{1,0:T(8,128)(2,1)S(1)}, bf16[120,1024]{1,0:T(8,128)(2,1)S(1)}, u32[]{:S(2)}, u32[]{:S(2)}) %collective-permute-start.4) | collective-permute-done | bytes 245792 | tf_op jit(solution)/shard_map/ppermute | solution.py:28
  113.9 0.9 copy-done.3
  114.9 1.5 fusion.40
  117.3 1.0 fusion.14
  118.3 8.4 %all-to-all-start.1 = ((f32[128,2,128]{2,1,0:T(2,128)}), f32[128,2,128]{2,1,0:T(2,128)S(1)}, u32[]{:S(2)}, u32[]{:S(2)}) async-start(f32[128,2,128]{2,1,0:T(2,128)} %bitcast.26), calls=%async_computation.1 | async-start | bytes 262144 | tf_op jit(solution)/shard_map/all_to_all | solution.py:109
  127.4 9.0 %all-to-all-done.1 = f32[128,2,128]{2,1,0:T(2,128)S(1)} async-done(((f32[128,2,128]{2,1,0:T(2,128)}), f32[128,2,128]{2,1,0:T(2,128)S(1)}, u32[]{:S(2)}, u32[]{:S(2)}) %all-to-all-start.1) | async-done | bytes 131104 | tf_op jit(solution)/shard_map/all_to_all | solution.py:109
  136.9 1.4 convolution_convert_fusion.1
  138.3 1.4 convolution_convert_fusion
  140.5 4.4 %all-to-all-start = ((bf16[32,16,384]{2,1,0:T(8,128)(2,1)}), bf16[32,16,384]{2,1,0:T(8,128)(2,1)S(1)}, u32[]{:S(2)}, u32[]{:S(2)}) async-start(bf16[32,16,384]{2,1,0:T(8,128)(2,1)} %pad_maximum_fusion), calls=%async_computation | async-start | bytes 786432 | tf_op jit(solution)/shard_map/all_to_all | solution.py:169
  145.0 10.4 %all-to-all-done = bf16[32,16,384]{2,1,0:T(8,128)(2,1)S(1)} async-done(((bf16[32,16,384]{2,1,0:T(8,128)(2,1)}), bf16[32,16,384]{2,1,0:T(8,128)(2,1)S(1)}, u32[]{:S(2)}, u32[]{:S(2)}) %all-to-all-start) | async-done | bytes 393248 | tf_op jit(solution)/shard_map/all_to_all | solution.py:169
  155.4 0.9 collective-permute-start.12
  156.4 1.3 collective-permute-start.11
  157.7 4.3 %collective-permute-done.10 = f32[16,384]{1,0:T(8,128)S(1)} collective-permute-done((f32[16,384]{1,0:T(8,128)S(1)}, f32[16,384]{1,0:T(8,128)S(1)}, u32[]{:S(2)}, u32[]{:S(2)}) %collective-permute-start.10) | collective-permute-done | bytes 24608 | tf_op jit(solution)/shard_map/ppermute | solution.py:28
  162.8 1.2 fusion.6
  164.1 2.0 fusion.5
  166.1 22.9 %all-gather.6.cloned.1.call-done = bf16[15360,512]{1,0:T(8,128)(2,1)} async-done(((bf16[480,512]{1,0:T(8,128)(2,1)}), bf16[15360,512]{1,0:T(8,128)(2,1)}) %all-gather.6.cloned.1.call-update) | async-done | bytes 15728656 | tf_op jit(solution)/shard_map/all_gather | solution.py:157
  189.0 5.5 %copy-done.1 = bf16[15360,512]{1,0:T(8,128)(2,1)S(1)} copy-done((bf16[15360,512]{1,0:T(8,128)(2,1)S(1)}, bf16[15360,512]{1,0:T(8,128)(2,1)}, u32[]{:S(2)}) %copy-start.1) | copy-done | bytes 15728664
  194.4 21.6 %shard_map.145 = bf16[4,32,2,128,128]{4,3,2,1,0:T(8,128)(2,1)} custom-call(s32[32,8]{1,0:T(8,128)S(1)} %add_select_fusion.1.blocks_ref, s32[32,8,128]{2,1,0:T(8,128)S(1)} %fusion.20.index_ref, bf16[32,480,512]{2,1,0:T(8,128)(2,1)S(1)} %bitcast.94), custom_call_target="tpu_custom_call" | custom-call | flops 4026531840 | bytes 25000000 | tf_op jit(solution)/shard_map/pallas_call | solution.py:69
  (66 shorter events, 9.6 us)
Async XLA Ops:
  7.2 1.3 copy-start
  7.2 59.6 %all-gather.4.cloned.1.call-start = ((), (), s32[]{:S(2)}) async-start(), calls=%async_computation.2 | async-start | bytes 8110080 | tf_op jit(solution)/shard_map/all_gather | solution.py:136
  11.0 177.9 %all-gather.6.cloned.1.call-start = ((), (), s32[]{:S(2)}) async-start(), calls=%async_computation.3 | async-start | bytes 16220160 | tf_op jit(solution)/shard_map/all_gather | solution.py:157
  11.1 70.2 %collective-permute-start.6 = (bf16[120,1024]{1,0:T(8,128)(2,1)}, bf16[120,1024]{1,0:T(8,128)(2,1)S(1)}, u32[]{:S(2)}, u32[]{:S(2)}) collective-permute-start(bf16[120,1024]{1,0:T(8,128)(2,1)} %pad_maximum_fusion.1), channel_id=1, source_target_pairs={{0,0},{4,1},{8,2},{12,3},{16,4},{20,5},{24,6},{28,7},{32,8},{36,9}... | collective-permute-start | bytes 737288 | tf_op jit(solution)/shard_map/ppermute | solution.py:142
  76.1 0.9 copy-start.4
  76.1 41.0 %copy-start.7 = (s32[192,1]{0,1:T(1,128)S(1)}, s32[192,1]{0,1:T(1,128)}, u32[]{:S(2)}) copy-start(s32[192,1]{0,1:T(1,128)} %param.16) | copy-start | bytes 2308
  76.1 41.2 %copy-start.8 = (s32[192]{0:T(256)S(1)}, s32[192]{0:T(256)}, u32[]{:S(2)}) copy-start(s32[192]{0:T(256)} %param.18) | copy-start | bytes 2308
  76.1 41.2 %copy-start.6 = (s32[192,128]{1,0:T(8,128)S(1)}, s32[192,128]{1,0:T(8,128)}, u32[]{:S(2)}) copy-start(s32[192,128]{1,0:T(8,128)} %param.17) | copy-start | bytes 294916
  76.1 50.6 %copy-start.2 = (f32[512,512]{1,0:T(8,128)S(1)}, f32[512,512]{1,0:T(8,128)}, u32[]{:S(2)}) copy-start(f32[512,512]{1,0:T(8,128)} %param.12) | copy-start | bytes 3145732
  77.1 8.6 %collective-permute-start = (bf16[120,1024]{1,0:T(8,128)(2,1)S(1)}, bf16[120,1024]{1,0:T(8,128)(2,1)S(1)}, u32[]{:S(2)}, u32[]{:S(2)}) collective-permute-start(bf16[120,1024]{1,0:T(8,128)(2,1)S(1)} %get-tuple-element.13), channel_id=1, source_target_pairs={{0,32},{32,64},{64,96},{96,0},{1,33},{33,65},{65,97},{97,1},{2,34}... | collective-permute-start | bytes 737288 | tf_op jit(solution)/shard_map/ppermute | solution.py:28
  78.3 7.4 %collective-permute-start.2 = (bf16[120,1024]{1,0:T(8,128)(2,1)S(1)}, bf16[120,1024]{1,0:T(8,128)(2,1)}, u32[]{:S(2)}, u32[]{:S(2)}) collective-permute-start(bf16[120,1024]{1,0:T(8,128)(2,1)S(1)} %get-tuple-element.14), channel_id=1, source_target_pairs={{0,96},{32,0},{64,32},{96,64},{1,97},{33,1},{65,33},{97,65},{2,98}... | collective-permute-start | bytes 737288 | tf_op jit(solution)/shard_map/ppermute | solution.py:28
  79.8 12.2 %collective-permute-start.1 = (bf16[120,1024]{1,0:T(8,128)(2,1)S(1)}, bf16[120,1024]{1,0:T(8,128)(2,1)}, u32[]{:S(2)}, u32[]{:S(2)}) collective-permute-start(bf16[120,1024]{1,0:T(8,128)(2,1)S(1)} %get-tuple-element.15), channel_id=1, source_target_pairs={{0,64},{32,96},{64,0},{96,32},{1,65},{33,97},{65,1},{97,33},{2,66}... | collective-permute-start | bytes 737288 | tf_op jit(solution)/shard_map/ppermute | solution.py:28
  81.3 31.7 %collective-permute-start.9 = (bf16[120,1024]{1,0:T(8,128)(2,1)S(1)}, bf16[120,1024]{1,0:T(8,128)(2,1)S(1)}, u32[]{:S(2)}, u32[]{:S(2)}) collective-permute-start(bf16[120,1024]{1,0:T(8,128)(2,1)S(1)} %collective-permute-done.6), channel_id=1, source_target_pairs={{0,96},{32,0},{64,32},{96,64},{1,97},{33,1},{65,33},{97,65},{2,98}... | collective-permute-start | bytes 737288 | tf_op jit(solution)/shard_map/ppermute | solution.py:28
  82.2 21.4 %collective-permute-start.8 = (bf16[120,1024]{1,0:T(8,128)(2,1)S(1)}, bf16[120,1024]{1,0:T(8,128)(2,1)S(1)}, u32[]{:S(2)}, u32[]{:S(2)}) collective-permute-start(bf16[120,1024]{1,0:T(8,128)(2,1)S(1)} %collective-permute-done.6), channel_id=1, source_target_pairs={{0,64},{32,96},{64,0},{96,32},{1,65},{33,97},{65,1},{97,33},{2,66}... | collective-permute-start | bytes 737288 | tf_op jit(solution)/shard_map/ppermute | solution.py:28
  85.6 0.7 copy-start.5
  85.6 17.3 %collective-permute-start.7 = (bf16[120,1024]{1,0:T(8,128)(2,1)S(1)}, bf16[120,1024]{1,0:T(8,128)(2,1)S(1)}, u32[]{:S(2)}, u32[]{:S(2)}) collective-permute-start(bf16[120,1024]{1,0:T(8,128)(2,1)S(1)} %collective-permute-done.6), channel_id=1, source_target_pairs={{0,32},{32,64},{64,96},{96,0},{1,33},{33,65},{65,97},{97,1},{2,34}... | collective-permute-start | bytes 737288 | tf_op jit(solution)/shard_map/ppermute | solution.py:28
  93.6 15.2 %collective-permute-start.3 = (bf16[120,1024]{1,0:T(8,128)(2,1)S(1)}, bf16[120,1024]{1,0:T(8,128)(2,1)S(1)}, u32[]{:S(2)}, u32[]{:S(2)}) collective-permute-start(bf16[120,1024]{1,0:T(8,128)(2,1)S(1)} %get-tuple-element.7), channel_id=1, source_target_pairs={{0,32},{32,64},{64,96},{96,0},{1,33},{33,65},{65,97},{97,1},{2,34}... | collective-permute-start | bytes 737288 | tf_op jit(solution)/shard_map/ppermute | solution.py:28
  103.0 10.0 %collective-permute-start.4 = (bf16[120,1024]{1,0:T(8,128)(2,1)S(1)}, bf16[120,1024]{1,0:T(8,128)(2,1)S(1)}, u32[]{:S(2)}, u32[]{:S(2)}) collective-permute-start(bf16[120,1024]{1,0:T(8,128)(2,1)S(1)} %get-tuple-element.7), channel_id=1, source_target_pairs={{0,64},{32,96},{64,0},{96,32},{1,65},{33,97},{65,1},{97,33},{2,66}... | collective-permute-start | bytes 737288 | tf_op jit(solution)/shard_map/ppermute | solution.py:28
  103.6 10.2 %collective-permute-start.5 = (bf16[120,1024]{1,0:T(8,128)(2,1)S(1)}, bf16[120,1024]{1,0:T(8,128)(2,1)S(1)}, u32[]{:S(2)}, u32[]{:S(2)}) collective-permute-start(bf16[120,1024]{1,0:T(8,128)(2,1)S(1)} %get-tuple-element.7), channel_id=1, source_target_pairs={{0,96},{32,0},{64,32},{96,64},{1,97},{33,1},{65,33},{97,65},{2,98}... | collective-permute-start | bytes 737288 | tf_op jit(solution)/shard_map/ppermute | solution.py:28
  113.9 0.9 copy-start.3
  118.3 18.1 %all-to-all-start.1 = ((f32[128,2,128]{2,1,0:T(2,128)}), f32[128,2,128]{2,1,0:T(2,128)S(1)}, u32[]{:S(2)}, u32[]{:S(2)}) async-start(f32[128,2,128]{2,1,0:T(2,128)} %bitcast.26), calls=%async_computation.1 | async-start | bytes 262144 | tf_op jit(solution)/shard_map/all_to_all | solution.py:109
  140.5 14.9 %all-to-all-start = ((bf16[32,16,384]{2,1,0:T(8,128)(2,1)}), bf16[32,16,384]{2,1,0:T(8,128)(2,1)S(1)}, u32[]{:S(2)}, u32[]{:S(2)}) async-start(bf16[32,16,384]{2,1,0:T(8,128)(2,1)} %pad_maximum_fusion), calls=%async_computation | async-start | bytes 786432 | tf_op jit(solution)/shard_map/all_to_all | solution.py:169
  155.4 6.6 %collective-permute-start.12 = (f32[16,384]{1,0:T(8,128)S(1)}, f32[16,384]{1,0:T(8,128)S(1)}, u32[]{:S(2)}, u32[]{:S(2)}) collective-permute-start(f32[16,384]{1,0:T(8,128)S(1)} %convert_reduce_fusion), channel_id=1, source_target_pairs={{0,96},{32,0},{64,32},{96,64},{1,97},{33,1},{65,33},{97,65},{2,98}... | collective-permute-start | bytes 73736 | tf_op jit(solution)/shard_map/ppermute | solution.py:28
  156.4 5.6 %collective-permute-start.11 = (f32[16,384]{1,0:T(8,128)S(1)}, f32[16,384]{1,0:T(8,128)S(1)}, u32[]{:S(2)}, u32[]{:S(2)}) collective-permute-start(f32[16,384]{1,0:T(8,128)S(1)} %convert_reduce_fusion), channel_id=1, source_target_pairs={{0,64},{32,96},{64,0},{96,32},{1,65},{33,97},{65,1},{97,33},{2,66}... | collective-permute-start | bytes 73736 | tf_op jit(solution)/shard_map/ppermute | solution.py:28
  157.7 4.3 %collective-permute-start.10 = (f32[16,384]{1,0:T(8,128)S(1)}, f32[16,384]{1,0:T(8,128)S(1)}, u32[]{:S(2)}, u32[]{:S(2)}) collective-permute-start(f32[16,384]{1,0:T(8,128)S(1)} %convert_reduce_fusion), channel_id=1, source_target_pairs={{0,32},{32,64},{64,96},{96,0},{1,33},{33,65},{65,97},{97,1},{2,34}... | collective-permute-start | bytes 73736 | tf_op jit(solution)/shard_map/ppermute | solution.py:28
  189.0 5.5 %copy-start.1 = (bf16[15360,512]{1,0:T(8,128)(2,1)S(1)}, bf16[15360,512]{1,0:T(8,128)(2,1)}, u32[]{:S(2)}) copy-start(bf16[15360,512]{1,0:T(8,128)(2,1)} %all-gather.6.cloned.1.call-done) | copy-start | bytes 47185924
Sparse Core Ops, SparseCore 0:
  11.2 55.5 all-gather.3
  116.5 72.3 all-gather.5

commit v2 on v1

v2 whole, which is shorter than its diff:
```python
import functools

import jax
import jax.numpy as jnp
from jax import lax
from jax.experimental import pallas as pl
from jax.experimental.pallas import tpu as pltpu
from jax.sharding import PartitionSpec as P

P_SIZE = 512
TILE = 128
TILE_CAP = 2
SIDE = 4
CODE = 512


def precise(left, right):
    return jnp.dot(left, right, precision=lax.Precision.HIGHEST, preferred_element_type=jnp.float32)


def contract_rows(left, right):
    return lax.dot_general(
        left, right, (((0,), (0,)), ((), ())), preferred_element_type=jnp.float32
    )


def place(block, received, index, dim):
    size = len(received) + 1
    shape = block.shape[:dim] + (size,) + block.shape[dim:]
    out = jnp.zeros(shape, block.dtype)
    out = lax.dynamic_update_index_in_dim(out, block, index, dim)
    for step, value in received:
        out = lax.dynamic_update_index_in_dim(out, value, (index - step) % size, dim)
    return out


def shift_rows(value, step):
    size = lax.axis_size("row")
    return lax.ppermute(value, "row", [(i, (i + step) % size) for i in range(size)])


def spread_rows(block):
    size = lax.axis_size("row")
    received = [(step, shift_rows(block, step)) for step in range(1, size)]
    return place(block, received, lax.axis_index("row"), 0)


def sum_rows(parts):
    size = lax.axis_size("row")
    row = lax.axis_index("row")
    total = lax.dynamic_index_in_dim(parts, row, 0, keepdims=False).astype(jnp.float32)
    for step in range(1, size):
        there = lax.dynamic_index_in_dim(parts, (row + step) % size, 0, keepdims=False)
        total = total + shift_rows(there, step).astype(jnp.float32)
    return total


def shift_chips(value, dim, step):
    perm = []
    for col in range(lax.axis_size("col")):
        place_of = [col // (2 * SIDE), col // 2 % SIDE, col % 2]
        place_of[dim] = (place_of[dim] + step) % SIDE
        perm.append((col, (place_of[0] * SIDE + place_of[1]) * 2 + place_of[2]))
    return lax.ppermute(value, "col", perm)


def spread_chips(block, dim, at):
    col = lax.axis_index("col")
    index = col // (2 * SIDE) if dim == 0 else col // 2 % SIDE
    received = [(step, shift_chips(block, dim, step)) for step in range(1, SIDE)]
    return place(block, received, index, at)


def spread_cores(block, at):
    size = lax.axis_size("col")
    other = lax.ppermute(block, "col", [(i, i ^ 1) for i in range(size)])
    return place(block, [(1, other)], lax.axis_index("col") % 2, at)


def spread_cols(block):
    half = block.shape[1] // 2
    left = spread_chips(spread_chips(block[:, :half], 1, 0), 0, 0)
    right = spread_chips(spread_chips(block[:, half:], 0, 0), 1, 1)
    return spread_cores(left, 2), spread_cores(right, 2)


def tile_kernel(blocks_ref, index_ref, band_ref, out_ref):
    pieces, group, piece_rows = band_ref.shape[:3]
    senders, _, slots = out_ref.shape[:3]
    first = pl.program_id(0) * group
    places = lax.broadcasted_iota(jnp.int32, (TILE, pieces * piece_rows), 1)
    for band in range(group):
        columns = index_ref[band].T
        for sender in range(senders):
            for slot in range(slots):
                k = sender * slots + slot
                pick = jnp.where(columns[:, k : k + 1] == places, 1.0, 0.0).astype(jnp.bfloat16)
                start = pl.multiple_of(blocks_ref[first + band, k] * TILE, TILE)
                rows = [band_ref[piece, band, :, pl.ds(start, TILE)] for piece in range(pieces)]
                out_ref[sender, band, slot] = jnp.dot(
                    pick, jnp.concatenate(rows, axis=0), preferred_element_type=jnp.float32
                ).astype(jnp.bfloat16)


def build_tiles(blocks, index, bands):
    pieces, col_count, piece_rows, width = bands.shape
    row_count = index.shape[1] // TILE_CAP
    group = 8
    return pl.pallas_call(
        tile_kernel,
        grid_spec=pltpu.PrefetchScalarGridSpec(
            num_scalar_prefetch=1,
            grid=(col_count // group,),
            in_specs=[
                pl.BlockSpec((group, row_count * TILE_CAP, TILE), lambda b, _: (b, 0, 0)),
                pl.BlockSpec((pieces, group, piece_rows, width), lambda b, _: (0, b, 0, 0)),
            ],
            out_specs=pl.BlockSpec(
                (row_count, group, TILE_CAP, TILE, TILE), lambda b, _: (0, b, 0, 0, 0)
            ),
        ),
        out_shape=jax.ShapeDtypeStruct(
            (row_count, col_count, TILE_CAP, TILE, TILE), jnp.bfloat16
        ),
        compiler_params=pltpu.CompilerParams(vmem_limit_bytes=56 * 1024 * 1024),
        cost_estimate=pl.CostEstimate(
            flops=512 * TILE * TILE * pieces * piece_rows,
            bytes_accessed=25_000_000,
            transcendentals=0,
        ),
    )(blocks, index, bands)


def route_indices(tile_owner, tile_rows, tile_block, tile_count, device_count):
    tile_total = tile_rows.shape[0]
    owners = tile_owner[:, 0]
    order_ids = jnp.arange(tile_total, dtype=jnp.int32)
    live = order_ids < tile_count[0]
    earlier = (
        (owners[:, None] == owners[None, :])
        & live[None, :]
        & (order_ids[None, :] < order_ids[:, None])
    )
    slots = jnp.sum(earlier.astype(jnp.int32), axis=1)
    dump = device_count * TILE_CAP
    target = jnp.where(live, owners * TILE_CAP + slots, dump)
    table = (target[None, :] == jnp.arange(dump, dtype=jnp.int32)[:, None]).astype(jnp.float32)
    coded = jnp.where(tile_rows >= 0, tile_rows + 1 + CODE * tile_block[:, None], 0)
    placed = precise(table, coded.astype(jnp.float32))
    return placed.reshape(device_count, TILE_CAP, TILE)


def shards(
    trailing,
    first_panel,
    first_gram,
    second_panel,
    second_lead,
    second_gram,
    tile_owner,
    tile_rows,
    tile_block,
    tile_count,
):
    row_count = lax.axis_size("row")
    col_count = lax.axis_size("col")
    row_index = lax.axis_index("row")
    col_index = lax.axis_index("col")
    device_count = row_count * col_count
    part_rows = first_panel.shape[0]
    gram_rows = P_SIZE // col_count
    low = jnp.bfloat16

    rest = (second_panel - precise(first_panel, second_lead)).astype(low)
    left, right = spread_cols(rest)
    first_low, _ = lax.optimization_barrier((first_panel.astype(low), rest))
    first_rows = lax.all_gather(first_low, "col", axis=0, tiled=True)

    perm = []
    for there in range(device_count):
        row, col = divmod(there, col_count)
        perm.append((col * row_count + row, there))
    own = lax.ppermute(jnp.concatenate([first_low, rest], axis=1), ("row", "col"), perm)

    trailing_low = lax.optimization_barrier(trailing.astype(low))

    def product(*factors):
        parts = [-contract_rows(trailing_low, f.reshape(-1, f.shape[-1])) for f in factors]
        whole = jnp.concatenate(parts, axis=1) if len(parts) > 1 else parts[0]
        return whole.astype(low).reshape(row_count, part_rows, P_SIZE)

    second_part = sum_rows(product(left, right)).astype(low)
    second_low = spread_rows(second_part).reshape(-1, P_SIZE)
    second_column = second_low.astype(jnp.float32)
    bands = lax.all_gather(second_low, "col", axis=0, tiled=False)

    first_rows, own, _ = lax.optimization_barrier((first_rows, own, second_low))
    lists = route_indices(tile_owner, tile_rows, tile_block, tile_count, device_count)
    first_product, lists = lax.optimization_barrier((product(first_rows), lists))
    first_part = sum_rows(first_product).astype(low)
    coded = lax.all_to_all(lists, ("row", "col"), split_axis=0, concat_axis=0, tiled=True)
    first_low_column = spread_rows(first_part).reshape(-1, P_SIZE)
    first_column = first_low_column.astype(jnp.float32)
    own = spread_rows(own).reshape(-1, 2 * P_SIZE)

    gram_start = col_index * gram_rows
    gram_part = lax.dynamic_slice_in_dim(first_gram, gram_start, gram_rows, 0)
    lead_part = lax.dynamic_slice_in_dim(second_lead, gram_start, gram_rows, 1)
    upper_part = precise(gram_part, second_lead)
    corner_part = lax.dynamic_slice_in_dim(second_gram, gram_start, gram_rows, 0) + precise(
        precise(lead_part.T, first_gram), second_lead
    )

    width = P_SIZE // row_count
    start = row_index * width
    first_cut = lax.dynamic_slice_in_dim(first_low_column, start, width, 1)
    second_cut = lax.dynamic_slice_in_dim(second_low, start, width, 1)
    against_first = contract_rows(
        own[:, :P_SIZE], jnp.concatenate([first_cut, second_cut], axis=1)
    )
    against_second = contract_rows(own[:, P_SIZE:], second_cut)
    sums = jnp.concatenate([against_first, against_second], axis=1).astype(low)
    sums = sums.reshape(col_count, gram_rows, 3 * width)
    sums = lax.all_to_all(sums, "col", split_axis=0, concat_axis=0, tiled=True)
    sums = jnp.sum(sums.astype(jnp.float32), axis=0)
    bands, sums, upper_part, corner_part = lax.optimization_barrier(
        (bands, sums, upper_part, corner_part)
    )
    sums = spread_rows(sums).reshape(row_count, gram_rows, 3, width)
    sums = sums.transpose(1, 2, 0, 3).reshape(gram_rows, 3 * P_SIZE)

    coded = coded.astype(jnp.int32).reshape(row_count, col_count, TILE_CAP, TILE)
    coded = coded.transpose(1, 0, 2, 3).reshape(col_count, row_count * TILE_CAP, TILE)
    tiles = build_tiles(coded[:, :, 0] // CODE, coded % CODE - 1, bands[None])
    child_tiles = tiles.reshape(device_count * TILE_CAP, TILE, TILE)

    first_corner = gram_part - sums[:, :P_SIZE]
    second_upper = -(upper_part + sums[:, P_SIZE : 2 * P_SIZE])
    second_corner = corner_part - sums[:, 2 * P_SIZE :]
    return (first_column, first_corner, second_upper, second_column, second_corner, child_tiles)


def solution(mesh):
    in_specs = (
        P("row", "col"),
        P(("row", "col"), None),
        P(),
        P(("row", "col"), None),
        P(),
        P(),
        P(("row", "col"), None),
        P(("row", "col"), None),
        P(("row", "col")),
        P(("row", "col")),
    )
    out_specs = (
        P("col", None),
        P("col", None),
        P("col", None),
        P("col", None),
        P("col", None),
        P(("row", "col"), None, None),
    )
    return jax.shard_map(shards, mesh=mesh, in_specs=in_specs, out_specs=out_specs, check_vma=False)
```

time: 223 us -> 188 us (0.84)
  waiting for transfers between devices: 124 us -> 34.8 us
  starting transfers between devices: 27.7 us -> 73.5 us
  other arithmetic: 6.53 us -> 14.6 us
  local copies, waits for them, and re-layouts: 9.2 us -> 16.8 us
  Pallas kernels: 21.6 us -> 15.8 us
  matrix products: 18.8 us -> 15.9 us
    all_gather x1, waiting for transfers between devices: 51.1 us -> 0.01 us  [shards(): first_rows = lax.all_gather(first_low, 'col', axis=0, tiled=True)]
    ppermute x1 -> x15, starting transfers between devices: 4.51 us -> 28.1 us  [the longest x12 15.9 us: shift_chips(): return lax.ppermute(value, 'col', perm)]
    all_gather x1, waiting for transfers between devices: 22.9 us -> 0.02 us  [shards(): bands = lax.all_gather(second_low, 'col', axis=0, tiled=False)]
    ppermute x12 -> x18, waiting for transfers between devices: 30.5 us -> 14.2 us  [shift_rows(): lax.ppermute(value, 'row', [(i, (i + step) % size) for i in range(size)])]
    ppermute x12 -> x18, starting transfers between devices: 10.3 us -> 22.8 us  [shift_rows(): lax.ppermute(value, 'row', [(i, (i + step) % size) for i in range(size)])]
    dynamic_update_slice x10 -> x33, local copies, waits for them, and re-layouts: 0.17 us -> 11.8 us  [the longest x25 9.07 us: place(): lax.dynamic_update_index_in_dim(out, value, (index - step) % size, dim)]
    convert_element_type x0 -> x4, other arithmetic: none -> 9.31 us  [the longest x1 5.42 us: shards(): trailing_low = lax.optimization_barrier(trailing.astype(low))]
    ppermute x1 -> x15, waiting for transfers between devices: 0.01 us -> 8.98 us  [the longest x12 8.97 us: shift_chips(): return lax.ppermute(value, 'col', perm)]
  transfers between devices with their start and end apart: 17 -> 37, of which waited for: 11 -> 14; matrix products, arithmetic and copies ran while one was open for 10% -> 22% of each run, Pallas kernels for 0% -> 8%
where the time goes in v2:
time: 188 us; the launch traced here: 187 us
  starting transfers between devices  73.5 us (39%)
  waiting for transfers between devices  34.8 us (19%)
  local copies, waits for them, and re-layouts  16.8 us (9%)
  matrix products  15.9 us (8%)
  Pallas kernels  15.8 us (8%)
  between operations  15.4 us (8%)
  other arithmetic  14.6 us (8%)
    ppermute x18, starting transfers between devices, shift_rows(): lax.ppermute(value, 'row', [(i, (i + step) % size) for i in range(size)])  22.8 us
    ppermute x12, starting transfers between devices, shift_chips(): return lax.ppermute(value, 'col', perm)  15.9 us
    pallas_call x1, Pallas kernels, build_tiles(): pl.pallas_call(tile_kernel, grid_spec=pltpu.PrefetchScalarGridSpec(num_sc...  15.8 us
    ppermute x18, waiting for transfers between devices, shift_rows(): lax.ppermute(value, 'row', [(i, (i + step) % size) for i in range(size)])  14.2 us
    all_to_all x1, starting transfers between devices, shards(): lax.all_to_all(lists, ('row', 'col'), split_axis=0, concat_axis=0, tiled=...  11.6 us
    all_to_all x1, starting transfers between devices, shards(): sums = lax.all_to_all(sums, 'col', split_axis=0, concat_axis=0, tiled=True)  11 us
    dot_general x5, matrix products, contract_rows(): lax.dot_general(left, right, (((0,), (0,)), ((), ())), preferred_element_...  10.4 us
    dynamic_update_slice x25, local copies, waits for them, and re-layouts, place(): lax.dynamic_update_index_in_dim(out, value, (index - step) % size, dim)  9.07 us
  transfers between devices with their start and end apart: 37, of which 14 were waited for; matrix products, arithmetic and copies ran while one was open for 22% of the time, Pallas kernels for 8%

profile of v2, /device:TPU:1, one launch (start us, length us, event | category | flops | bytes accessed | tf_op | source)
XLA Modules:
  0.0 186.8 jit_solution(7138458672226438624)
XLA Ops:
  7.2 1.7 convert_element_type.74
  8.9 1.8 fusion.3
  10.8 2.5 %collective-permute-start.1 = (bf16[120,256]{1,0:T(8,128)(2,1)S(1)}, bf16[120,256]{1,0:T(8,128)(2,1)S(1)}, u32[]{:S(2)}, u32[]{:S(2)}) collective-permute-start(bf16[120,256]{1,0:T(8,128)(2,1)S(1)} %get-tuple-element.35), channel_id=1, source_target_pairs={{0,2},{1,3},{2,4},{3,5},{4,6},{5,7},{6,0},{7,1},{8,10},{9,11},{10,... | collective-permute-start | bytes 184328 | tf_op jit(solution)/shard_map/ppermute | solution.py:64
  13.3 3.3 %collective-permute-start.2 = (bf16[120,256]{1,0:T(8,128)(2,1)S(1)}, bf16[120,256]{1,0:T(8,128)(2,1)S(1)}, u32[]{:S(2)}, u32[]{:S(2)}) collective-permute-start(bf16[120,256]{1,0:T(8,128)(2,1)S(1)} %get-tuple-element.35), channel_id=1, source_target_pairs={{0,4},{1,5},{2,6},{3,7},{4,0},{5,1},{6,2},{7,3},{8,12},{9,13},{10,... | collective-permute-start | bytes 184328 | tf_op jit(solution)/shard_map/ppermute | solution.py:64
  18.7 2.6 %collective-permute-start.9 = (bf16[120,256]{1,0:T(8,128)(2,1)S(1)}, bf16[120,256]{1,0:T(8,128)(2,1)S(1)}, u32[]{:S(2)}, u32[]{:S(2)}) collective-permute-start(bf16[120,256]{1,0:T(8,128)(2,1)S(1)} %get-tuple-element.34), channel_id=1, source_target_pairs={{0,16},{1,17},{2,18},{3,19},{4,20},{5,21},{6,22},{7,23},{8,24},{9,... | collective-permute-start | bytes 184328 | tf_op jit(solution)/shard_map/ppermute | solution.py:64
  25.1 1.7 collective-permute-start.6
  31.2 3.1 %collective-permute-done.4 = bf16[4,120,256]{2,1,0:T(8,128)(2,1)S(1)} collective-permute-done((bf16[4,120,256]{2,1,0:T(8,128)(2,1)S(1)}, bf16[4,120,256]{2,1,0:T(8,128)(2,1)S(1)}, u32[]{:S(2)}, u32[]{:S(2)}) %collective-permute-start.4) | collective-permute-done | bytes 245792 | tf_op jit(solution)/shard_map/ppermute | solution.py:64
  34.3 2.0 %collective-permute-done.5 = bf16[4,120,256]{2,1,0:T(8,128)(2,1)S(1)} collective-permute-done((bf16[4,120,256]{2,1,0:T(8,128)(2,1)S(1)}, bf16[4,120,256]{2,1,0:T(8,128)(2,1)S(1)}, u32[]{:S(2)}, u32[]{:S(2)}) %collective-permute-start.5) | collective-permute-done | bytes 245792 | tf_op jit(solution)/shard_map/ppermute | solution.py:64
  36.3 2.7 %collective-permute-done.6 = bf16[4,120,256]{2,1,0:T(8,128)(2,1)S(1)} collective-permute-done((bf16[4,120,256]{2,1,0:T(8,128)(2,1)S(1)}, bf16[4,120,256]{2,1,0:T(8,128)(2,1)S(1)}, u32[]{:S(2)}, u32[]{:S(2)}) %collective-permute-start.6) | collective-permute-done | bytes 245792 | tf_op jit(solution)/shard_map/ppermute | solution.py:64
  39.1 2.1 %collective-permute-start.7 = (bf16[4,4,120,256]{3,2,1,0:T(8,128)(2,1)S(1)}, bf16[4,4,120,256]{3,2,1,0:T(8,128)(2,1)}, u32[]{:S(2)}, u32[]{:S(2)}) collective-permute-start(bf16[4,4,120,256]{3,2,1,0:T(8,128)(2,1)S(1)} %bitcast_dynamic-update-slice_fusion.12), channel_id=1, source_target_pairs={{0,1},{1,0},{2,3},{3,2},{4,5},{5,4},{6,7},{7,6},{8,9},{9,8},{10,11... | collective-permute-start | bytes 2949128 | tf_op jit(solution)/shard_map/ppermute | solution.py:76
  42.4 4.8 %collective-permute-start.14 = (bf16[4,4,120,256]{3,2,1,0:T(8,128)(2,1)S(1)}, bf16[4,4,120,256]{3,2,1,0:T(8,128)(2,1)}, u32[]{:S(2)}, u32[]{:S(2)}) collective-permute-start(bf16[4,4,120,256]{3,2,1,0:T(8,128)(2,1)S(1)} %bitcast_dynamic-update-slice_fusion.4), channel_id=1, source_target_pairs={{0,1},{1,0},{2,3},{3,2},{4,5},{5,4},{6,7},{7,6},{8,9},{9,8},{10,11... | collective-permute-start | bytes 2949128 | tf_op jit(solution)/shard_map/ppermute | solution.py:76
  47.2 5.4 %convert_element_type.76 = bf16[3840,480]{0,1:T(8,128)(2,1)} convert(f32[3840,480]{0,1:T(8,128)} %param.10) | non-fusion elementwise | flops 1843200 | bytes 11059200 | tf_op jit(solution)/shard_map/convert_element_type | solution.py:185
  53.1 1.9 %bitcast_dynamic-update-slice_fusion = (bf16[4,4,2,120,256]{4,3,2,1,0:T(8,128)(2,1)S(1)}, bf16[4,4,2,120,256]{4,3,2,1,0:T(8,128)(2,1)S(1)}) fusion(bf16[4,4,2,120,256]{4,3,2,1,0:T(8,128)(2,1)S(1)} %bitcast_dynamic-update-slice_fusion.1, s32[]{:T(128)S(6)} %select_n.252, bf16[4,4,120,256]{3,2,1,0:T(8,128)(2,1)} %collective-permute-done.14, ...), kind=kLoop, calls=%fused_computation.11 | loop fusion | bytes 3932164 | tf_op jit(solution)/shard_map/jit(dynamic_update_index_in_dim)/dynamic_update_slice | solution.py:33
  59.8 2.4 %collective-permute-start.16 = (bf16[120,512]{1,0:T(8,128)(2,1)S(1)}, bf16[120,512]{1,0:T(8,128)(2,1)S(1)}, u32[]{:S(2)}, u32[]{:S(2)}) collective-permute-start(bf16[120,512]{1,0:T(8,128)(2,1)S(1)} %get-tuple-element.32), channel_id=1, source_target_pairs={{0,64},{32,96},{64,0},{96,32},{1,65},{33,97},{65,1},{97,33},{2,66}... | collective-permute-start | bytes 368648 | tf_op jit(solution)/shard_map/ppermute | solution.py:39
  64.2 3.9 %collective-permute-done.16 = bf16[120,512]{1,0:T(8,128)(2,1)S(1)} collective-permute-done((bf16[120,512]{1,0:T(8,128)(2,1)S(1)}, bf16[120,512]{1,0:T(8,128)(2,1)S(1)}, u32[]{:S(2)}, u32[]{:S(2)}) %collective-permute-start.16) | collective-permute-done | bytes 122912 | tf_op jit(solution)/shard_map/ppermute | solution.py:39
  70.0 2.4 %collective-permute-start.19 = (bf16[120,512]{1,0:T(8,128)(2,1)S(1)}, bf16[120,512]{1,0:T(8,128)(2,1)S(1)}, u32[]{:S(2)}, u32[]{:S(2)}) collective-permute-start(bf16[120,512]{1,0:T(8,128)(2,1)S(1)} %get-tuple-element.27), channel_id=1, source_target_pairs={{0,64},{32,96},{64,0},{96,32},{1,65},{33,97},{65,1},{97,33},{2,66}... | collective-permute-start | bytes 368648 | tf_op jit(solution)/shard_map/ppermute | solution.py:39
  73.6 2.0 %collective-permute-done.18 = bf16[120,512]{1,0:T(8,128)(2,1)S(1)} collective-permute-done((bf16[120,512]{1,0:T(8,128)(2,1)S(1)}, bf16[120,512]{1,0:T(8,128)(2,1)S(1)}, u32[]{:S(2)}, u32[]{:S(2)}) %collective-permute-start.18) | collective-permute-done | bytes 122912 | tf_op jit(solution)/shard_map/ppermute | solution.py:39
  78.8 5.3 %collective-permute-start = (bf16[120,1024]{1,0:T(8,128)(2,1)S(1)}, bf16[120,1024]{1,0:T(8,128)(2,1)}, u32[]{:S(2)}, u32[]{:S(2)}) collective-permute-start(bf16[120,1024]{1,0:T(8,128)(2,1)S(1)} %pad_maximum_fusion.1), channel_id=1, source_target_pairs={{0,0},{4,1},{8,2},{12,3},{16,4},{20,5},{24,6},{28,7},{32,8},{36,9}... | collective-permute-start | bytes 737288 | tf_op jit(solution)/shard_map/ppermute | solution.py:183
  90.7 3.9 %collective-permute-start.28 = (bf16[120,1024]{1,0:T(8,128)(2,1)}, bf16[120,1024]{1,0:T(8,128)(2,1)}, u32[]{:S(2)}, u32[]{:S(2)}) collective-permute-start(bf16[120,1024]{1,0:T(8,128)(2,1)} %collective-permute-done), channel_id=1, source_target_pairs={{0,64},{32,96},{64,0},{96,32},{1,65},{33,97},{65,1},{97,33},{2,66}... | collective-permute-start | bytes 737288 | tf_op jit(solution)/shard_map/ppermute | solution.py:39
  94.6 5.4 %fusion = bf16[512,480]{0,1:T(8,128)(2,1)S(1)} fusion(bf16[3840,480]{0,1:T(8,128)(2,1)} %convert_element_type.76, bf16[3840,512]{1,0:T(8,128)(2,1)} %all-gather.3.cloned.1.call-done), kind=kOutput, calls=%fused_computation.1 | convolution fusion | flops 1887928320 | bytes 8110080 | tf_op jit(solution)/shard_map/dot_general | solution.py:22
  100.4 2.4 %collective-permute-start.23 = (bf16[120,512]{1,0:T(8,128)(2,1)S(1)}, bf16[120,512]{1,0:T(8,128)(2,1)}, u32[]{:S(2)}, u32[]{:S(2)}) collective-permute-start(bf16[120,512]{1,0:T(8,128)(2,1)S(1)} %get-tuple-element.29), channel_id=1, source_target_pairs={{0,96},{32,0},{64,32},{96,64},{1,97},{33,1},{65,33},{97,65},{2,98}... | collective-permute-start | bytes 368648 | tf_op jit(solution)/shard_map/ppermute | solution.py:39
  102.8 11.6 %all-to-all-start.1 = ((f32[128,2,128]{2,1,0:T(2,128)}), f32[128,2,128]{2,1,0:T(2,128)S(1)}, u32[]{:S(2)}, u32[]{:S(2)}) async-start(f32[128,2,128]{2,1,0:T(2,128)} %bitcast.46), calls=%async_computation.1 | async-start | bytes 262144 | tf_op jit(solution)/shard_map/all_to_all | solution.py:201
  115.5 2.7 %collective-permute-start.29 = (bf16[120,1024]{1,0:T(8,128)(2,1)}, bf16[120,1024]{1,0:T(8,128)(2,1)}, u32[]{:S(2)}, u32[]{:S(2)}) collective-permute-start(bf16[120,1024]{1,0:T(8,128)(2,1)} %collective-permute-done), channel_id=1, source_target_pairs={{0,96},{32,0},{64,32},{96,64},{1,97},{33,1},{65,33},{97,65},{2,98}... | collective-permute-start | bytes 737288 | tf_op jit(solution)/shard_map/ppermute | solution.py:39
  119.4 1.7 collective-permute-start.25
  121.1 3.0 %all-to-all-done.1 = f32[128,2,128]{2,1,0:T(2,128)S(1)} async-done(((f32[128,2,128]{2,1,0:T(2,128)}), f32[128,2,128]{2,1,0:T(2,128)S(1)}, u32[]{:S(2)}, u32[]{:S(2)}) %all-to-all-start.1) | async-done | bytes 131104 | tf_op jit(solution)/shard_map/all_to_all | solution.py:201
  126.5 3.9 %collective-permute-done.26 = bf16[120,512]{1,0:T(8,128)(2,1)S(1)} collective-permute-done((bf16[120,512]{1,0:T(8,128)(2,1)S(1)}, bf16[120,512]{1,0:T(8,128)(2,1)S(1)}, u32[]{:S(2)}, u32[]{:S(2)}) %collective-permute-start.26) | collective-permute-done | bytes 122912 | tf_op jit(solution)/shard_map/ppermute | solution.py:39
  130.5 1.7 bitcast_dynamic-update-slice_fusion.10
  132.2 1.7 bitcast_dynamic-update-slice_fusion.9
  139.1 11.0 %all-to-all-start = ((bf16[32,16,384]{2,1,0:T(8,128)(2,1)}), bf16[32,16,384]{2,1,0:T(8,128)(2,1)S(1)}, u32[]{:S(2)}, u32[]{:S(2)}) async-start(bf16[32,16,384]{2,1,0:T(8,128)(2,1)} %pad_maximum_fusion), calls=%async_computation | async-start | bytes 786432 | tf_op jit(solution)/shard_map/all_to_all | solution.py:224
  151.8 8.6 %all-to-all-done = bf16[32,16,384]{2,1,0:T(8,128)(2,1)S(1)} async-done(((bf16[32,16,384]{2,1,0:T(8,128)(2,1)}), bf16[32,16,384]{2,1,0:T(8,128)(2,1)S(1)}, u32[]{:S(2)}, u32[]{:S(2)}) %all-to-all-start) | async-done | bytes 393248 | tf_op jit(solution)/shard_map/all_to_all | solution.py:224
  160.5 2.0 %collective-permute-start.31 = (f32[16,384]{1,0:T(8,128)S(1)}, f32[16,384]{1,0:T(8,128)S(1)}, u32[]{:S(2)}, u32[]{:S(2)}) collective-permute-start(f32[16,384]{1,0:T(8,128)S(1)} %convert_reduce_fusion), channel_id=1, source_target_pairs={{0,64},{32,96},{64,0},{96,32},{1,65},{33,97},{65,1},{97,33},{2,66}... | collective-permute-start | bytes 73736 | tf_op jit(solution)/shard_map/ppermute | solution.py:39
  163.2 15.8 %shard_map.145 = bf16[4,32,2,128,128]{4,3,2,1,0:T(8,128)(2,1)} custom-call(s32[32,8]{1,0:T(8,128)} %add_select_fusion.1.blocks_ref, s32[32,8,128]{2,1,0:T(8,128)} %fusion.20.index_ref, bf16[1,32,480,512]{3,2,1,0:T(8,128)(2,1)} %bitcast.173), custom_call_target="tpu_custom_call" | custom-call | flops 4026531840 | bytes 25000000 | tf_op jit(solution)/shard_map/pallas_call | solution.py:109
  (150 shorter events, 44.4 us)
Async XLA Ops:
  7.2 83.2 %all-gather.3.cloned.1.call-start = ((), (), s32[]{:S(2)}) async-start(), calls=%async_computation.2 | async-start | bytes 4055040 | tf_op jit(solution)/shard_map/all_gather | solution.py:177
  10.7 149.7 %all-gather.5.cloned.1.call-start = ((), (), s32[]{:S(2)}) async-start(), calls=%async_computation.3 | async-start | bytes 16220160 | tf_op jit(solution)/shard_map/all_gather | solution.py:195
  10.8 11.9 %collective-permute-start.1 = (bf16[120,256]{1,0:T(8,128)(2,1)S(1)}, bf16[120,256]{1,0:T(8,128)(2,1)S(1)}, u32[]{:S(2)}, u32[]{:S(2)}) collective-permute-start(bf16[120,256]{1,0:T(8,128)(2,1)S(1)} %get-tuple-element.35), channel_id=1, source_target_pairs={{0,2},{1,3},{2,4},{3,5},{4,6},{5,7},{6,0},{7,1},{8,10},{9,11},{10,... | collective-permute-start | bytes 184328 | tf_op jit(solution)/shard_map/ppermute | solution.py:64
  13.3 10.4 %collective-permute-start.2 = (bf16[120,256]{1,0:T(8,128)(2,1)S(1)}, bf16[120,256]{1,0:T(8,128)(2,1)S(1)}, u32[]{:S(2)}, u32[]{:S(2)}) collective-permute-start(bf16[120,256]{1,0:T(8,128)(2,1)S(1)} %get-tuple-element.35), channel_id=1, source_target_pairs={{0,4},{1,5},{2,6},{3,7},{4,0},{5,1},{6,2},{7,3},{8,12},{9,13},{10,... | collective-permute-start | bytes 184328 | tf_op jit(solution)/shard_map/ppermute | solution.py:64
  16.6 7.1 %collective-permute-start.3 = (bf16[120,256]{1,0:T(8,128)(2,1)S(1)}, bf16[120,256]{1,0:T(8,128)(2,1)S(1)}, u32[]{:S(2)}, u32[]{:S(2)}) collective-permute-start(bf16[120,256]{1,0:T(8,128)(2,1)S(1)} %get-tuple-element.35), channel_id=1, source_target_pairs={{0,6},{1,7},{2,0},{3,1},{4,2},{5,3},{6,4},{7,5},{8,14},{9,15},{10,... | collective-permute-start | bytes 184328 | tf_op jit(solution)/shard_map/ppermute | solution.py:64
  17.4 7.7 %collective-permute-start.8 = (bf16[120,256]{1,0:T(8,128)(2,1)S(1)}, bf16[120,256]{1,0:T(8,128)(2,1)S(1)}, u32[]{:S(2)}, u32[]{:S(2)}) collective-permute-start(bf16[120,256]{1,0:T(8,128)(2,1)S(1)} %get-tuple-element.34), channel_id=1, source_target_pairs={{0,8},{1,9},{2,10},{3,11},{4,12},{5,13},{6,14},{7,15},{8,16},{9,17... | collective-permute-start | bytes 184328 | tf_op jit(solution)/shard_map/ppermute | solution.py:64
  18.7 8.7 %collective-permute-start.9 = (bf16[120,256]{1,0:T(8,128)(2,1)S(1)}, bf16[120,256]{1,0:T(8,128)(2,1)S(1)}, u32[]{:S(2)}, u32[]{:S(2)}) collective-permute-start(bf16[120,256]{1,0:T(8,128)(2,1)S(1)} %get-tuple-element.34), channel_id=1, source_target_pairs={{0,16},{1,17},{2,18},{3,19},{4,20},{5,21},{6,22},{7,23},{8,24},{9,... | collective-permute-start | bytes 184328 | tf_op jit(solution)/shard_map/ppermute | solution.py:64
  23.8 10.5 %collective-permute-start.4 = (bf16[4,120,256]{2,1,0:T(8,128)(2,1)S(1)}, bf16[4,120,256]{2,1,0:T(8,128)(2,1)S(1)}, u32[]{:S(2)}, u32[]{:S(2)}) collective-permute-start(bf16[4,120,256]{2,1,0:T(8,128)(2,1)S(1)} %bitcast_dynamic-update-slice_fusion.28), channel_id=1, source_target_pairs={{0,8},{1,9},{2,10},{3,11},{4,12},{5,13},{6,14},{7,15},{8,16},{9,17... | collective-permute-start | bytes 737288 | tf_op jit(solution)/shard_map/ppermute | solution.py:64
  24.3 12.1 %collective-permute-start.5 = (bf16[4,120,256]{2,1,0:T(8,128)(2,1)S(1)}, bf16[4,120,256]{2,1,0:T(8,128)(2,1)S(1)}, u32[]{:S(2)}, u32[]{:S(2)}) collective-permute-start(bf16[4,120,256]{2,1,0:T(8,128)(2,1)S(1)} %bitcast_dynamic-update-slice_fusion.28), channel_id=1, source_target_pairs={{0,16},{1,17},{2,18},{3,19},{4,20},{5,21},{6,22},{7,23},{8,24},{9,... | collective-permute-start | bytes 737288 | tf_op jit(solution)/shard_map/ppermute | solution.py:64
  25.1 14.0 %collective-permute-start.6 = (bf16[4,120,256]{2,1,0:T(8,128)(2,1)S(1)}, bf16[4,120,256]{2,1,0:T(8,128)(2,1)S(1)}, u32[]{:S(2)}, u32[]{:S(2)}) collective-permute-start(bf16[4,120,256]{2,1,0:T(8,128)(2,1)S(1)} %bitcast_dynamic-update-slice_fusion.28), channel_id=1, source_target_pairs={{0,24},{1,25},{2,26},{3,27},{4,28},{5,29},{6,30},{7,31},{8,0},{9,1... | collective-permute-start | bytes 737288 | tf_op jit(solution)/shard_map/ppermute | solution.py:64
  28.6 12.5 %collective-permute-start.11 = (bf16[4,120,256]{2,1,0:T(8,128)(2,1)}, bf16[4,120,256]{2,1,0:T(8,128)(2,1)S(1)}, u32[]{:S(2)}, u32[]{:S(2)}) collective-permute-start(bf16[4,120,256]{2,1,0:T(8,128)(2,1)} %bitcast_dynamic-update-slice_fusion.24), channel_id=1, source_target_pairs={{0,2},{1,3},{2,4},{3,5},{4,6},{5,7},{6,0},{7,1},{8,10},{9,11},{10,... | collective-permute-start | bytes 737288 | tf_op jit(solution)/shard_map/ppermute | solution.py:64
  29.4 11.8 %collective-permute-start.12 = (bf16[4,120,256]{2,1,0:T(8,128)(2,1)}, bf16[4,120,256]{2,1,0:T(8,128)(2,1)S(1)}, u32[]{:S(2)}, u32[]{:S(2)}) collective-permute-start(bf16[4,120,256]{2,1,0:T(8,128)(2,1)} %bitcast_dynamic-update-slice_fusion.24), channel_id=1, source_target_pairs={{0,4},{1,5},{2,6},{3,7},{4,0},{5,1},{6,2},{7,3},{8,12},{9,13},{10,... | collective-permute-start | bytes 737288 | tf_op jit(solution)/shard_map/ppermute | solution.py:64
  34.3 8.1 %collective-permute-start.13 = (bf16[4,120,256]{2,1,0:T(8,128)(2,1)}, bf16[4,120,256]{2,1,0:T(8,128)(2,1)S(1)}, u32[]{:S(2)}, u32[]{:S(2)}) collective-permute-start(bf16[4,120,256]{2,1,0:T(8,128)(2,1)} %bitcast_dynamic-update-slice_fusion.24), channel_id=1, source_target_pairs={{0,6},{1,7},{2,0},{3,1},{4,2},{5,3},{6,4},{7,5},{8,14},{9,15},{10,... | collective-permute-start | bytes 737288 | tf_op jit(solution)/shard_map/ppermute | solution.py:64
  39.1 14.0 %collective-permute-start.7 = (bf16[4,4,120,256]{3,2,1,0:T(8,128)(2,1)S(1)}, bf16[4,4,120,256]{3,2,1,0:T(8,128)(2,1)}, u32[]{:S(2)}, u32[]{:S(2)}) collective-permute-start(bf16[4,4,120,256]{3,2,1,0:T(8,128)(2,1)S(1)} %bitcast_dynamic-update-slice_fusion.12), channel_id=1, source_target_pairs={{0,1},{1,0},{2,3},{3,2},{4,5},{5,4},{6,7},{7,6},{8,9},{9,8},{10,11... | collective-permute-start | bytes 2949128 | tf_op jit(solution)/shard_map/ppermute | solution.py:76
  42.4 10.8 %collective-permute-start.14 = (bf16[4,4,120,256]{3,2,1,0:T(8,128)(2,1)S(1)}, bf16[4,4,120,256]{3,2,1,0:T(8,128)(2,1)}, u32[]{:S(2)}, u32[]{:S(2)}) collective-permute-start(bf16[4,4,120,256]{3,2,1,0:T(8,128)(2,1)S(1)} %bitcast_dynamic-update-slice_fusion.4), channel_id=1, source_target_pairs={{0,1},{1,0},{2,3},{3,2},{4,5},{5,4},{6,7},{7,6},{8,9},{9,8},{10,11... | collective-permute-start | bytes 2949128 | tf_op jit(solution)/shard_map/ppermute | solution.py:76
  59.8 8.3 %collective-permute-start.16 = (bf16[120,512]{1,0:T(8,128)(2,1)S(1)}, bf16[120,512]{1,0:T(8,128)(2,1)S(1)}, u32[]{:S(2)}, u32[]{:S(2)}) collective-permute-start(bf16[120,512]{1,0:T(8,128)(2,1)S(1)} %get-tuple-element.32), channel_id=1, source_target_pairs={{0,64},{32,96},{64,0},{96,32},{1,65},{33,97},{65,1},{97,33},{2,66}... | collective-permute-start | bytes 368648 | tf_op jit(solution)/shard_map/ppermute | solution.py:39
  62.2 5.9 %collective-permute-start.17 = (bf16[120,512]{1,0:T(8,128)(2,1)S(1)}, bf16[120,512]{1,0:T(8,128)(2,1)}, u32[]{:S(2)}, u32[]{:S(2)}) collective-permute-start(bf16[120,512]{1,0:T(8,128)(2,1)S(1)} %get-tuple-element.33), channel_id=1, source_target_pairs={{0,96},{32,0},{64,32},{96,64},{1,97},{33,1},{65,33},{97,65},{2,98}... | collective-permute-start | bytes 368648 | tf_op jit(solution)/shard_map/ppermute | solution.py:39
  70.0 7.1 %collective-permute-start.19 = (bf16[120,512]{1,0:T(8,128)(2,1)S(1)}, bf16[120,512]{1,0:T(8,128)(2,1)S(1)}, u32[]{:S(2)}, u32[]{:S(2)}) collective-permute-start(bf16[120,512]{1,0:T(8,128)(2,1)S(1)} %get-tuple-element.27), channel_id=1, source_target_pairs={{0,64},{32,96},{64,0},{96,32},{1,65},{33,97},{65,1},{97,33},{2,66}... | collective-permute-start | bytes 368648 | tf_op jit(solution)/shard_map/ppermute | solution.py:39
  78.8 11.7 %collective-permute-start = (bf16[120,1024]{1,0:T(8,128)(2,1)S(1)}, bf16[120,1024]{1,0:T(8,128)(2,1)}, u32[]{:S(2)}, u32[]{:S(2)}) collective-permute-start(bf16[120,1024]{1,0:T(8,128)(2,1)S(1)} %pad_maximum_fusion.1), channel_id=1, source_target_pairs={{0,0},{4,1},{8,2},{12,3},{16,4},{20,5},{24,6},{28,7},{32,8},{36,9}... | collective-permute-start | bytes 737288 | tf_op jit(solution)/shard_map/ppermute | solution.py:183
  90.4 40.1 %collective-permute-start.27 = (bf16[120,1024]{1,0:T(8,128)(2,1)}, bf16[120,1024]{1,0:T(8,128)(2,1)}, u32[]{:S(2)}, u32[]{:S(2)}) collective-permute-start(bf16[120,1024]{1,0:T(8,128)(2,1)} %collective-permute-done), channel_id=1, source_target_pairs={{0,32},{32,64},{64,96},{96,0},{1,33},{33,65},{65,97},{97,1},{2,34}... | collective-permute-start | bytes 737288 | tf_op jit(solution)/shard_map/ppermute | solution.py:39
  90.7 41.5 %collective-permute-start.28 = (bf16[120,1024]{1,0:T(8,128)(2,1)}, bf16[120,1024]{1,0:T(8,128)(2,1)}, u32[]{:S(2)}, u32[]{:S(2)}) collective-permute-start(bf16[120,1024]{1,0:T(8,128)(2,1)} %collective-permute-done), channel_id=1, source_target_pairs={{0,64},{32,96},{64,0},{96,32},{1,65},{33,97},{65,1},{97,33},{2,66}... | collective-permute-start | bytes 737288 | tf_op jit(solution)/shard_map/ppermute | solution.py:39
  100.0 15.5 %collective-permute-start.21 = (bf16[120,512]{1,0:T(8,128)(2,1)S(1)}, bf16[120,512]{1,0:T(8,128)(2,1)S(1)}, u32[]{:S(2)}, u32[]{:S(2)}) collective-permute-start(bf16[120,512]{1,0:T(8,128)(2,1)S(1)} %get-tuple-element.28), channel_id=1, source_target_pairs={{0,32},{32,64},{64,96},{96,0},{1,33},{33,65},{65,97},{97,1},{2,34}... | collective-permute-start | bytes 368648 | tf_op jit(solution)/shard_map/ppermute | solution.py:39
  100.1 18.1 %collective-permute-start.22 = (bf16[120,512]{1,0:T(8,128)(2,1)S(1)}, bf16[120,512]{1,0:T(8,128)(2,1)}, u32[]{:S(2)}, u32[]{:S(2)}) collective-permute-start(bf16[120,512]{1,0:T(8,128)(2,1)S(1)} %get-tuple-element.30), channel_id=1, source_target_pairs={{0,64},{32,96},{64,0},{96,32},{1,65},{33,97},{65,1},{97,33},{2,66}... | collective-permute-start | bytes 368648 | tf_op jit(solution)/shard_map/ppermute | solution.py:39
  100.4 17.8 %collective-permute-start.23 = (bf16[120,512]{1,0:T(8,128)(2,1)S(1)}, bf16[120,512]{1,0:T(8,128)(2,1)}, u32[]{:S(2)}, u32[]{:S(2)}) collective-permute-start(bf16[120,512]{1,0:T(8,128)(2,1)S(1)} %get-tuple-element.29), channel_id=1, source_target_pairs={{0,96},{32,0},{64,32},{96,64},{1,97},{33,1},{65,33},{97,65},{2,98}... | collective-permute-start | bytes 368648 | tf_op jit(solution)/shard_map/ppermute | solution.py:39
  102.8 21.4 %all-to-all-start.1 = ((f32[128,2,128]{2,1,0:T(2,128)}), f32[128,2,128]{2,1,0:T(2,128)S(1)}, u32[]{:S(2)}, u32[]{:S(2)}) async-start(f32[128,2,128]{2,1,0:T(2,128)} %bitcast.46), calls=%async_computation.1 | async-start | bytes 262144 | tf_op jit(solution)/shard_map/all_to_all | solution.py:201
  115.5 18.3 %collective-permute-start.29 = (bf16[120,1024]{1,0:T(8,128)(2,1)}, bf16[120,1024]{1,0:T(8,128)(2,1)}, u32[]{:S(2)}, u32[]{:S(2)}) collective-permute-start(bf16[120,1024]{1,0:T(8,128)(2,1)} %collective-permute-done), channel_id=1, source_target_pairs={{0,96},{32,0},{64,32},{96,64},{1,97},{33,1},{65,33},{97,65},{2,98}... | collective-permute-start | bytes 737288 | tf_op jit(solution)/shard_map/ppermute | solution.py:39
  119.3 7.0 %collective-permute-start.24 = (bf16[120,512]{1,0:T(8,128)(2,1)S(1)}, bf16[120,512]{1,0:T(8,128)(2,1)S(1)}, u32[]{:S(2)}, u32[]{:S(2)}) collective-permute-start(bf16[120,512]{1,0:T(8,128)(2,1)S(1)} %get-tuple-element.25), channel_id=1, source_target_pairs={{0,32},{32,64},{64,96},{96,0},{1,33},{33,65},{65,97},{97,1},{2,34}... | collective-permute-start | bytes 368648 | tf_op jit(solution)/shard_map/ppermute | solution.py:39
  119.4 7.1 %collective-permute-start.25 = (bf16[120,512]{1,0:T(8,128)(2,1)S(1)}, bf16[120,512]{1,0:T(8,128)(2,1)S(1)}, u32[]{:S(2)}, u32[]{:S(2)}) collective-permute-start(bf16[120,512]{1,0:T(8,128)(2,1)S(1)} %get-tuple-element.25), channel_id=1, source_target_pairs={{0,64},{32,96},{64,0},{96,32},{1,65},{33,97},{65,1},{97,33},{2,66}... | collective-permute-start | bytes 368648 | tf_op jit(solution)/shard_map/ppermute | solution.py:39
  139.1 21.3 %all-to-all-start = ((bf16[32,16,384]{2,1,0:T(8,128)(2,1)}), bf16[32,16,384]{2,1,0:T(8,128)(2,1)S(1)}, u32[]{:S(2)}, u32[]{:S(2)}) async-start(bf16[32,16,384]{2,1,0:T(8,128)(2,1)} %pad_maximum_fusion), calls=%async_computation | async-start | bytes 786432 | tf_op jit(solution)/shard_map/all_to_all | solution.py:224
  160.5 18.6 %collective-permute-start.30 = (f32[16,384]{1,0:T(8,128)S(1)}, f32[16,384]{1,0:T(8,128)S(1)}, u32[]{:S(2)}, u32[]{:S(2)}) collective-permute-start(f32[16,384]{1,0:T(8,128)S(1)} %convert_reduce_fusion), channel_id=1, source_target_pairs={{0,32},{32,64},{64,96},{96,0},{1,33},{33,65},{65,97},{97,1},{2,34}... | collective-permute-start | bytes 73736 | tf_op jit(solution)/shard_map/ppermute | solution.py:39
  160.5 18.5 %collective-permute-start.31 = (f32[16,384]{1,0:T(8,128)S(1)}, f32[16,384]{1,0:T(8,128)S(1)}, u32[]{:S(2)}, u32[]{:S(2)}) collective-permute-start(f32[16,384]{1,0:T(8,128)S(1)} %convert_reduce_fusion), channel_id=1, source_target_pairs={{0,64},{32,96},{64,0},{96,32},{1,65},{33,97},{65,1},{97,33},{2,66}... | collective-permute-start | bytes 73736 | tf_op jit(solution)/shard_map/ppermute | solution.py:39
  162.5 16.6 %collective-permute-start.32 = (f32[16,384]{1,0:T(8,128)S(1)}, f32[16,384]{1,0:T(8,128)S(1)}, u32[]{:S(2)}, u32[]{:S(2)}) collective-permute-start(f32[16,384]{1,0:T(8,128)S(1)} %convert_reduce_fusion), channel_id=1, source_target_pairs={{0,96},{32,0},{64,32},{96,64},{1,97},{33,1},{65,33},{97,65},{2,98}... | collective-permute-start | bytes 73736 | tf_op jit(solution)/shard_map/ppermute | solution.py:39
  (18 other events, 194.3 us)
Sparse Core Ops, SparseCore 0:
  10.8 52.8 all-gather.2
  78.8 71.4 all-gather.4

commit v3 on v2

--- a/solution.py
+++ b/solution.py
@@ -22,6 +22,10 @@
     return lax.dot_general(
         left, right, (((0,), (0,)), ((), ())), preferred_element_type=jnp.float32
     )
+
+
+def after(value, *others):
+    return lax.optimization_barrier((value, *others))[0]
 
 
 def place(block, received, index, dim):
@@ -39,10 +43,12 @@
     return lax.ppermute(value, "row", [(i, (i + step) % size) for i in range(size)])
 
 
-def spread_rows(block):
-    size = lax.axis_size("row")
-    received = [(step, shift_rows(block, step)) for step in range(1, size)]
-    return place(block, received, lax.axis_index("row"), 0)
+def exchange_rows(block):
+    return [block] + [shift_rows(block, step) for step in range(1, lax.axis_size("row"))]
+
+
+def in_row_order(blocks):
+    return place(blocks[0], list(enumerate(blocks))[1:], lax.axis_index("row"), 0)
 
 
 def sum_rows(parts):
@@ -77,33 +83,29 @@
     return place(block, [(1, other)], lax.axis_index("col") % 2, at)
 
 
-def spread_cols(block):
+def spread_lines(block):
     half = block.shape[1] // 2
-    left = spread_chips(spread_chips(block[:, :half], 1, 0), 0, 0)
-    right = spread_chips(spread_chips(block[:, half:], 0, 0), 1, 1)
-    return spread_cores(left, 2), spread_cores(right, 2)
+    return spread_chips(block[:, :half], 1, 0), spread_chips(block[:, half:], 0, 0)
 
 
 def tile_kernel(blocks_ref, index_ref, band_ref, out_ref):
-    pieces, group, piece_rows = band_ref.shape[:3]
+    group, band_rows = band_ref.shape[:2]
     senders, _, slots = out_ref.shape[:3]
     first = pl.program_id(0) * group
-    places = lax.broadcasted_iota(jnp.int32, (TILE, pieces * piece_rows), 1)
+    places = lax.broadcasted_iota(jnp.int32, (band_rows, TILE), 0)
     for band in range(group):
-        columns = index_ref[band].T
         for sender in range(senders):
             for slot in range(slots):
                 k = sender * slots + slot
-                pick = jnp.where(columns[:, k : k + 1] == places, 1.0, 0.0).astype(jnp.bfloat16)
+                pick = jnp.where(index_ref[band, k : k + 1] == places, 1.0, 0.0)
                 start = pl.multiple_of(blocks_ref[first + band, k] * TILE, TILE)
-                rows = [band_ref[piece, band, :, pl.ds(start, TILE)] for piece in range(pieces)]
-                out_ref[sender, band, slot] = jnp.dot(
-                    pick, jnp.concatenate(rows, axis=0), preferred_element_type=jnp.float32
+                out_ref[sender, band, slot] = contract_rows(
+                    pick.astype(jnp.bfloat16), band_ref[band, :, pl.ds(start, TILE)]
                 ).astype(jnp.bfloat16)
 
 
 def build_tiles(blocks, index, bands):
-    pieces, col_count, piece_rows, width = bands.shape
+    col_count, band_rows, width = bands.shape
     row_count = index.shape[1] // TILE_CAP
     group = 8
     return pl.pallas_call(
@@ -113,7 +115,7 @@
             grid=(col_count // group,),
             in_specs=[
                 pl.BlockSpec((group, row_count * TILE_CAP, TILE), lambda b, _: (b, 0, 0)),
-                pl.BlockSpec((pieces, group, piece_rows, width), lambda b, _: (0, b, 0, 0)),
+                pl.BlockSpec((group, band_rows, width), lambda b, _: (b, 0, 0)),
             ],
             out_specs=pl.BlockSpec(
                 (row_count, group, TILE_CAP, TILE, TILE), lambda b, _: (0, b, 0, 0, 0)
@@ -124,7 +126,7 @@
         ),
         compiler_params=pltpu.CompilerParams(vmem_limit_bytes=56 * 1024 * 1024),
         cost_estimate=pl.CostEstimate(
-            flops=512 * TILE * TILE * pieces * piece_rows,
+            flops=512 * TILE * TILE * band_rows,
             bytes_accessed=25_000_000,
             transcendentals=0,
         ),
@@ -172,66 +174,72 @@
     low = jnp.bfloat16
 
     rest = (second_panel - precise(first_panel, second_lead)).astype(low)
-    left, right = spread_cols(rest)
-    first_low, _ = lax.optimization_barrier((first_panel.astype(low), rest))
+    left, right = spread_lines(rest)
+    first_low = after(first_panel, left).astype(low)
     first_rows = lax.all_gather(first_low, "col", axis=0, tiled=True)
+    left = spread_chips(left, 0, 0)
+    right = spread_chips(right, 1, 1)
+    right, trailing_low = lax.optimization_barrier((right, after(trailing, left).astype(low)))
+    left, right = spread_cores(left, 2), spread_cores(right, 2)
+
+    def product(*factors):
+        parts = [-contract_rows(trailing_low, f.reshape(-1, f.shape[-1])) for f in factors]
+        whole = jnp.concatenate(parts, axis=1) if len(parts) > 1 else parts[0]
+        return whole.astype(low).reshape(row_count, part_rows, P_SIZE)
+
+    second_part = sum_rows(product(left, right)).astype(low)
+    second_blocks = exchange_rows(second_part)
+    second_low = in_row_order(second_blocks).reshape(-1, P_SIZE)
+    bands = lax.all_gather(second_low, "col", axis=0, tiled=False)
 
     perm = []
     for there in range(device_count):
         row, col = divmod(there, col_count)
         perm.append((col * row_count + row, there))
-    own = lax.ppermute(jnp.concatenate([first_low, rest], axis=1), ("row", "col"), perm)
-
-    trailing_low = lax.optimization_barrier(trailing.astype(low))
-
-    def product(*factors):
-        parts = [-contract_rows(trailing_low, f.reshape(-1, f.shape[-1])) for f in factors]
-        whole = jnp.concatenate(parts, axis=1) if len(parts) > 1 else parts[0]
-        return whole.astype(low).reshape(row_count, part_rows, P_SIZE)
-
-    second_part = sum_rows(product(left, right)).astype(low)
-    second_low = spread_rows(second_part).reshape(-1, P_SIZE)
-    second_column = second_low.astype(jnp.float32)
-    bands = lax.all_gather(second_low, "col", axis=0, tiled=False)
-
-    first_rows, own, _ = lax.optimization_barrier((first_rows, own, second_low))
+    own = after(jnp.concatenate([first_low, rest], axis=1), second_part)
+    own = lax.ppermute(own, ("row", "col"), perm)
+
     lists = route_indices(tile_owner, tile_rows, tile_block, tile_count, device_count)
-    first_product, lists = lax.optimization_barrier((product(first_rows), lists))
+    first_product = product(after(first_rows, second_part))
+    first_product, lists = lax.optimization_barrier((first_product, lists))
     first_part = sum_rows(first_product).astype(low)
     coded = lax.all_to_all(lists, ("row", "col"), split_axis=0, concat_axis=0, tiled=True)
-    first_low_column = spread_rows(first_part).reshape(-1, P_SIZE)
-    first_column = first_low_column.astype(jnp.float32)
-    own = spread_rows(own).reshape(-1, 2 * P_SIZE)
-
+    own = jnp.concatenate(exchange_rows(after(own, first_product)), axis=0)
+    first_blocks = exchange_rows(first_part)
+
+    width = P_SIZE // row_count
+    start = row_index * width
+    cuts = [
+        jnp.concatenate([lax.dynamic_slice_in_dim(b, start, width, 1) for b in blocks], axis=0)
+        for blocks in (first_blocks, second_blocks)
+    ]
+    against_first = contract_rows(own[:, :P_SIZE], jnp.concatenate(cuts, axis=1))
+    against_second = contract_rows(own[:, P_SIZE:], cuts[1])
+    sums = jnp.concatenate([against_first, against_second], axis=1).astype(low)
+    sums = sums.reshape(col_count, gram_rows, 3 * width)
+    first_column = in_row_order(after(first_blocks, sums)).reshape(-1, P_SIZE).astype(jnp.float32)
+    second_column = after(second_low, sums).astype(jnp.float32)
+
+    lead = after(second_lead, sums)
     gram_start = col_index * gram_rows
     gram_part = lax.dynamic_slice_in_dim(first_gram, gram_start, gram_rows, 0)
-    lead_part = lax.dynamic_slice_in_dim(second_lead, gram_start, gram_rows, 1)
-    upper_part = precise(gram_part, second_lead)
+    lead_part = lax.dynamic_slice_in_dim(lead, gram_start, gram_rows, 1)
+    upper_part = precise(gram_part, lead)
     corner_part = lax.dynamic_slice_in_dim(second_gram, gram_start, gram_rows, 0) + precise(
-        precise(lead_part.T, first_gram), second_lead
-    )
-
-    width = P_SIZE // row_count
-    start = row_index * width
-    first_cut = lax.dynamic_slice_in_dim(first_low_column, start, width, 1)
-    second_cut = lax.dynamic_slice_in_dim(second_low, start, width, 1)
-    against_first = contract_rows(
-        own[:, :P_SIZE], jnp.concatenate([first_cut, second_cut], axis=1)
-    )
-    against_second = contract_rows(own[:, P_SIZE:], second_cut)
-    sums = jnp.concatenate([against_first, against_second], axis=1).astype(low)
-    sums = sums.reshape(col_count, gram_rows, 3 * width)
+        precise(lead_part.T, first_gram), lead
+    )
+
     sums = lax.all_to_all(sums, "col", split_axis=0, concat_axis=0, tiled=True)
     sums = jnp.sum(sums.astype(jnp.float32), axis=0)
     bands, sums, upper_part, corner_part = lax.optimization_barrier(
         (bands, sums, upper_part, corner_part)
     )
-    sums = spread_rows(sums).reshape(row_count, gram_rows, 3, width)
+    sums = in_row_order(exchange_rows(sums)).reshape(row_count, gram_rows, 3, width)
     sums = sums.transpose(1, 2, 0, 3).reshape(gram_rows, 3 * P_SIZE)
 
     coded = coded.astype(jnp.int32).reshape(row_count, col_count, TILE_CAP, TILE)
     coded = coded.transpose(1, 0, 2, 3).reshape(col_count, row_count * TILE_CAP, TILE)
-    tiles = build_tiles(coded[:, :, 0] // CODE, coded % CODE - 1, bands[None])
+    tiles = build_tiles(coded[:, :, 0] // CODE, coded % CODE - 1, bands)
     child_tiles = tiles.reshape(device_count * TILE_CAP, TILE, TILE)
 
     first_corner = gram_part - sums[:, :P_SIZE]

time: 188 us -> 182 us (0.968)
  waiting for transfers between devices: 34.8 us -> 41.9 us
  local copies, waits for them, and re-layouts: 16.8 us -> 12.4 us
  starting transfers between devices: 73.5 us -> 69.2 us
  other arithmetic: 14.6 us -> 11.4 us
    dynamic_update_slice x25 -> x22, local copies, waits for them, and re-layouts: 9.07 us -> 3.86 us  [place(): lax.dynamic_update_index_in_dim(out, value, (index - step) % size, dim)]
    all_to_all x1, starting transfers between devices: 11.6 us -> 7.17 us  [shards(): lax.all_to_all(lists, ('row', 'col'), split_axis=0, concat_axis=0, tiled=...]
    all_to_all x1, waiting for transfers between devices: 3.03 us -> 6.85 us  [shards(): lax.all_to_all(lists, ('row', 'col'), split_axis=0, concat_axis=0, tiled=...]
    ppermute x12, starting transfers between devices: 15.9 us -> 19.1 us  [shift_chips(): return lax.ppermute(value, 'col', perm)]
    ppermute x2, waiting for transfers between devices: 0.01 us -> 3.14 us  [spread_cores(): other = lax.ppermute(block, 'col', [(i, i ^ 1) for i in range(size)])]
    ppermute x12, waiting for transfers between devices: 8.97 us -> 6.49 us  [shift_chips(): return lax.ppermute(value, 'col', perm)]
    ppermute x2, starting transfers between devices: 6.88 us -> 4.58 us  [spread_cores(): other = lax.ppermute(block, 'col', [(i, i ^ 1) for i in range(size)])]
    dynamic_update_slice x2 -> x1, other arithmetic: 2.15 us -> 0.08 us  [place(): out = lax.dynamic_update_index_in_dim(out, block, index, dim)]
  transfers between devices with their start and end apart: 37 -> 37, of which waited for: 14 -> 13; matrix products, arithmetic and copies ran while one was open for 22% -> 19% of each run, Pallas kernels for 8% -> 8%
where the time goes in v3:
time: 182 us; the launch traced here: 181 us
  starting transfers between devices  69.2 us (38%)
  waiting for transfers between devices  41.9 us (23%)
  matrix products  16.1 us (9%)
  between operations  15.4 us (8%)
  Pallas kernels  14.8 us (8%)
  local copies, waits for them, and re-layouts  12.4 us (7%)
  other arithmetic  11.4 us (6%)
    ppermute x18, starting transfers between devices, shift_rows(): lax.ppermute(value, 'row', [(i, (i + step) % size) for i in range(size)])  24.5 us
    ppermute x12, starting transfers between devices, shift_chips(): return lax.ppermute(value, 'col', perm)  19.1 us
    ppermute x18, waiting for transfers between devices, shift_rows(): lax.ppermute(value, 'row', [(i, (i + step) % size) for i in range(size)])  16.3 us
    pallas_call x1, Pallas kernels, build_tiles(): pl.pallas_call(tile_kernel, grid_spec=pltpu.PrefetchScalarGridSpec(num_sc...  14.8 us
    dot_general x5, matrix products, contract_rows(): lax.dot_general(left, right, (((0,), (0,)), ((), ())), preferred_element_...  10.7 us
    all_to_all x1, waiting for transfers between devices, shards(): sums = lax.all_to_all(sums, 'col', split_axis=0, concat_axis=0, tiled=True)  9.05 us
    all_to_all x1, starting transfers between devices, shards(): sums = lax.all_to_all(sums, 'col', split_axis=0, concat_axis=0, tiled=True)  9.03 us
    all_to_all x1, starting transfers between devices, shards(): lax.all_to_all(lists, ('row', 'col'), split_axis=0, concat_axis=0, tiled=...  7.17 us
  transfers between devices with their start and end apart: 37, of which 13 were waited for; matrix products, arithmetic and copies ran while one was open for 19% of the time, Pallas kernels for 8%

profile of v3, /device:TPU:1, one launch (start us, length us, event | category | flops | bytes accessed | tf_op | source)
XLA Modules:
  0.0 181.2 jit_solution(14693667310738170773)
XLA Ops:
  8.4 1.8 fusion.3
  10.2 2.5 %collective-permute-start.6 = (bf16[120,256]{1,0:T(8,128)(2,1)S(1)}, bf16[120,256]{1,0:T(8,128)(2,1)S(1)}, u32[]{:S(2)}, u32[]{:S(2)}) collective-permute-start(bf16[120,256]{1,0:T(8,128)(2,1)S(1)} %get-tuple-element.52), channel_id=1, source_target_pairs={{0,2},{1,3},{2,4},{3,5},{4,6},{5,7},{6,0},{7,1},{8,10},{9,11},{10,... | collective-permute-start | bytes 184328 | tf_op jit(solution)/shard_map/ppermute | solution.py:70
  12.7 3.3 %collective-permute-start.7 = (bf16[120,256]{1,0:T(8,128)(2,1)S(1)}, bf16[120,256]{1,0:T(8,128)(2,1)S(1)}, u32[]{:S(2)}, u32[]{:S(2)}) collective-permute-start(bf16[120,256]{1,0:T(8,128)(2,1)S(1)} %get-tuple-element.52), channel_id=1, source_target_pairs={{0,4},{1,5},{2,6},{3,7},{4,0},{5,1},{6,2},{7,3},{8,12},{9,13},{10,... | collective-permute-start | bytes 184328 | tf_op jit(solution)/shard_map/ppermute | solution.py:70
  16.9 1.6 collective-permute-done.7
  21.5 2.6 %collective-permute-start.1 = (bf16[120,256]{1,0:T(8,128)(2,1)S(1)}, bf16[120,256]{1,0:T(8,128)(2,1)S(1)}, u32[]{:S(2)}, u32[]{:S(2)}) collective-permute-start(bf16[120,256]{1,0:T(8,128)(2,1)S(1)} %get-tuple-element.53), channel_id=1, source_target_pairs={{0,16},{1,17},{2,18},{3,19},{4,20},{5,21},{6,22},{7,23},{8,24},{9,... | collective-permute-start | bytes 184328 | tf_op jit(solution)/shard_map/ppermute | solution.py:70
  27.7 1.6 collective-permute-start.11
  31.2 3.1 %collective-permute-start.4 = (bf16[4,120,256]{2,1,0:T(8,128)(2,1)}, bf16[4,120,256]{2,1,0:T(8,128)(2,1)S(1)}, u32[]{:S(2)}, u32[]{:S(2)}) collective-permute-start(bf16[4,120,256]{2,1,0:T(8,128)(2,1)} %bitcast_dynamic-update-slice_fusion.24), channel_id=1, source_target_pairs={{0,4},{1,5},{2,6},{3,7},{4,0},{5,1},{6,2},{7,3},{8,12},{9,13},{10,... | collective-permute-start | bytes 737288 | tf_op jit(solution)/shard_map/ppermute | solution.py:70
  35.5 1.6 collective-permute-start.5
  37.2 4.0 %collective-permute-done.11 = bf16[4,120,256]{2,1,0:T(8,128)(2,1)S(1)} collective-permute-done((bf16[4,120,256]{2,1,0:T(8,128)(2,1)S(1)}, bf16[4,120,256]{2,1,0:T(8,128)(2,1)S(1)}, u32[]{:S(2)}, u32[]{:S(2)}) %collective-permute-start.11) | collective-permute-done | bytes 245792 | tf_op jit(solution)/shard_map/ppermute | solution.py:70
  41.2 5.3 %convert_element_type.75 = bf16[3840,480]{0,1:T(8,128)(2,1)} convert(f32[3840,480]{0,1:T(8,128)} %param.10) | non-fusion elementwise | flops 1843200 | bytes 11059200 | tf_op jit(solution)/shard_map/convert_element_type | solution.py:182
  46.6 4.5 %collective-permute-start.13 = (bf16[4,4,120,256]{3,2,1,0:T(8,128)(2,1)S(1)}, bf16[4,4,120,256]{3,2,1,0:T(8,128)(2,1)}, u32[]{:S(2)}, u32[]{:S(2)}) collective-permute-start(bf16[4,4,120,256]{3,2,1,0:T(8,128)(2,1)S(1)} %bitcast_dynamic-update-slice_fusion.4), channel_id=1, source_target_pairs={{0,1},{1,0},{2,3},{3,2},{4,5},{5,4},{6,7},{7,6},{8,9},{9,8},{10,11... | collective-permute-start | bytes 2949128 | tf_op jit(solution)/shard_map/ppermute | solution.py:82
  51.7 1.7 collective-permute-done.13
  54.8 1.7 bitcast_dynamic-update-slice_fusion
  60.2 2.5 %collective-permute-start.15 = (bf16[120,512]{1,0:T(8,128)(2,1)S(1)}, bf16[120,512]{1,0:T(8,128)(2,1)S(1)}, u32[]{:S(2)}, u32[]{:S(2)}) collective-permute-start(bf16[120,512]{1,0:T(8,128)(2,1)S(1)} %get-tuple-element.50), channel_id=1, source_target_pairs={{0,64},{32,96},{64,0},{96,32},{1,65},{33,97},{65,1},{97,33},{2,66}... | collective-permute-start | bytes 368648 | tf_op jit(solution)/shard_map/ppermute | solution.py:43
  64.8 3.5 %collective-permute-done.15 = bf16[120,512]{1,0:T(8,128)(2,1)S(1)} collective-permute-done((bf16[120,512]{1,0:T(8,128)(2,1)S(1)}, bf16[120,512]{1,0:T(8,128)(2,1)S(1)}, u32[]{:S(2)}, u32[]{:S(2)}) %collective-permute-start.15) | collective-permute-done | bytes 122912 | tf_op jit(solution)/shard_map/ppermute | solution.py:43
  69.6 1.6 collective-permute-start.29
  73.5 3.4 %collective-permute-done.28 = bf16[120,512]{1,0:T(8,128)(2,1)S(1)} collective-permute-done((bf16[120,512]{1,0:T(8,128)(2,1)S(1)}, bf16[120,512]{1,0:T(8,128)(2,1)S(1)}, u32[]{:S(2)}, u32[]{:S(2)}) %collective-permute-start.28) | collective-permute-done | bytes 122912 | tf_op jit(solution)/shard_map/ppermute | solution.py:43
  79.7 4.7 %collective-permute-start.23 = (bf16[120,1024]{1,0:T(8,128)(2,1)S(1)}, bf16[120,1024]{1,0:T(8,128)(2,1)S(1)}, u32[]{:S(2)}, u32[]{:S(2)}) collective-permute-start(bf16[120,1024]{1,0:T(8,128)(2,1)S(1)} %pad_maximum_fusion.1), channel_id=1, source_target_pairs={{0,0},{4,1},{8,2},{12,3},{16,4},{20,5},{24,6},{28,7},{32,8},{36,9}... | collective-permute-start | bytes 737288 | tf_op jit(solution)/shard_map/ppermute | solution.py:200
  84.5 5.6 %fusion = bf16[480,512]{1,0:T(8,128)(2,1)S(1)} fusion(bf16[3840,480]{0,1:T(8,128)(2,1)} %convert_element_type.75, bf16[3840,512]{1,0:T(8,128)(2,1)} %all-gather.3.cloned.1.call-done), kind=kOutput, calls=%fused_computation.1 | convolution fusion | flops 1887928320 | bytes 8110080 | tf_op jit(solution)/shard_map/dot_general | solution.py:22
  90.1 1.6 collective-permute-start.17
  91.7 2.8 %collective-permute-start.18 = (bf16[120,512]{1,0:T(8,128)(2,1)S(1)}, bf16[120,512]{1,0:T(8,128)(2,1)S(1)}, u32[]{:S(2)}, u32[]{:S(2)}) collective-permute-start(bf16[120,512]{1,0:T(8,128)(2,1)S(1)} %get-tuple-element.48), channel_id=1, source_target_pairs={{0,64},{32,96},{64,0},{96,32},{1,65},{33,97},{65,1},{97,33},{2,66}... | collective-permute-start | bytes 368648 | tf_op jit(solution)/shard_map/ppermute | solution.py:43
  94.5 2.0 %collective-permute-start.19 = (bf16[120,512]{1,0:T(8,128)(2,1)S(1)}, bf16[120,512]{1,0:T(8,128)(2,1)S(1)}, u32[]{:S(2)}, u32[]{:S(2)}) collective-permute-start(bf16[120,512]{1,0:T(8,128)(2,1)S(1)} %get-tuple-element.47), channel_id=1, source_target_pairs={{0,96},{32,0},{64,32},{96,64},{1,97},{33,1},{65,33},{97,65},{2,98}... | collective-permute-start | bytes 368648 | tf_op jit(solution)/shard_map/ppermute | solution.py:43
  97.8 7.2 %all-to-all-start.1 = ((f32[128,2,128]{2,1,0:T(2,128)}), f32[128,2,128]{2,1,0:T(2,128)S(1)}, u32[]{:S(2)}, u32[]{:S(2)}) async-start(f32[128,2,128]{2,1,0:T(2,128)} %bitcast.38), calls=%async_computation.1 | async-start | bytes 262144 | tf_op jit(solution)/shard_map/all_to_all | solution.py:206
  105.7 2.6 %collective-permute-start.26 = (bf16[120,1024]{1,0:T(8,128)(2,1)S(1)}, bf16[120,1024]{1,0:T(8,128)(2,1)S(1)}, u32[]{:S(2)}, u32[]{:S(2)}) collective-permute-start(bf16[120,1024]{1,0:T(8,128)(2,1)S(1)} %collective-permute-done.23), channel_id=1, source_target_pairs={{0,96},{32,0},{64,32},{96,64},{1,97},{33,1},{65,33},{97,65},{2,98}... | collective-permute-start | bytes 737288 | tf_op jit(solution)/shard_map/ppermute | solution.py:43
  109.1 6.8 %all-to-all-done.1 = f32[128,2,128]{2,1,0:T(2,128)S(1)} async-done(((f32[128,2,128]{2,1,0:T(2,128)}), f32[128,2,128]{2,1,0:T(2,128)S(1)}, u32[]{:S(2)}, u32[]{:S(2)}) %all-to-all-start.1) | async-done | bytes 131104 | tf_op jit(solution)/shard_map/all_to_all | solution.py:206
  118.4 6.3 %collective-permute-done.20 = bf16[120,512]{1,0:T(8,128)(2,1)S(1)} collective-permute-done((bf16[120,512]{1,0:T(8,128)(2,1)S(1)}, bf16[120,512]{1,0:T(8,128)(2,1)S(1)}, u32[]{:S(2)}, u32[]{:S(2)}) %collective-permute-start.20) | collective-permute-done | bytes 122912 | tf_op jit(solution)/shard_map/ppermute | solution.py:43
  128.3 1.4 convolution_convert_fusion
  130.5 9.0 %all-to-all-start = ((bf16[32,16,384]{2,1,0:T(8,128)(2,1)}), bf16[32,16,384]{2,1,0:T(8,128)(2,1)S(1)}, u32[]{:S(2)}, u32[]{:S(2)}) async-start(bf16[32,16,384]{2,1,0:T(8,128)(2,1)} %pad_maximum_fusion), calls=%async_computation | async-start | bytes 786432 | tf_op jit(solution)/shard_map/all_to_all | solution.py:232
  144.6 9.1 %all-to-all-done = bf16[32,16,384]{2,1,0:T(8,128)(2,1)S(1)} async-done(((bf16[32,16,384]{2,1,0:T(8,128)(2,1)}), bf16[32,16,384]{2,1,0:T(8,128)(2,1)S(1)}, u32[]{:S(2)}, u32[]{:S(2)}) %all-to-all-start) | async-done | bytes 393248 | tf_op jit(solution)/shard_map/all_to_all | solution.py:232
  153.7 1.5 collective-permute-start.30
  155.2 2.1 %collective-permute-start.31 = (f32[16,384]{1,0:T(8,128)S(1)}, f32[16,384]{1,0:T(8,128)S(1)}, u32[]{:S(2)}, u32[]{:S(2)}) collective-permute-start(f32[16,384]{1,0:T(8,128)S(1)} %convert_reduce_fusion), channel_id=1, source_target_pairs={{0,64},{32,96},{64,0},{96,32},{1,65},{33,97},{65,1},{97,33},{2,66}... | collective-permute-start | bytes 73736 | tf_op jit(solution)/shard_map/ppermute | solution.py:43
  158.6 14.8 %shard_map.145 = bf16[4,32,2,128,128]{4,3,2,1,0:T(8,128)(2,1)} custom-call(s32[32,8]{1,0:T(8,128)} %add_select_fusion.1.blocks_ref, s32[32,8,128]{2,1,0:T(8,128)} %fusion.32.index_ref, bf16[32,480,512]{2,1,0:T(8,128)(2,1)} %all-gather.5.cloned.1.call-done.band_ref), custom_call_target="tpu_custom_call" | custom-call | flops 4026531840 | bytes 25000000 | tf_op jit(solution)/shard_map/pallas_call | solution.py:111
  (150 shorter events, 42.0 us)
Async XLA Ops:
  7.2 77.3 %all-gather.3.cloned.1.call-start = ((), (), s32[]{:S(2)}) async-start(), calls=%async_computation.2 | async-start | bytes 4055040 | tf_op jit(solution)/shard_map/all_gather | solution.py:179
  10.2 6.7 %collective-permute-start.6 = (bf16[120,256]{1,0:T(8,128)(2,1)S(1)}, bf16[120,256]{1,0:T(8,128)(2,1)S(1)}, u32[]{:S(2)}, u32[]{:S(2)}) collective-permute-start(bf16[120,256]{1,0:T(8,128)(2,1)S(1)} %get-tuple-element.52), channel_id=1, source_target_pairs={{0,2},{1,3},{2,4},{3,5},{4,6},{5,7},{6,0},{7,1},{8,10},{9,11},{10,... | collective-permute-start | bytes 184328 | tf_op jit(solution)/shard_map/ppermute | solution.py:70
  12.7 5.7 %collective-permute-start.7 = (bf16[120,256]{1,0:T(8,128)(2,1)S(1)}, bf16[120,256]{1,0:T(8,128)(2,1)S(1)}, u32[]{:S(2)}, u32[]{:S(2)}) collective-permute-start(bf16[120,256]{1,0:T(8,128)(2,1)S(1)} %get-tuple-element.52), channel_id=1, source_target_pairs={{0,4},{1,5},{2,6},{3,7},{4,0},{5,1},{6,2},{7,3},{8,12},{9,13},{10,... | collective-permute-start | bytes 184328 | tf_op jit(solution)/shard_map/ppermute | solution.py:70
  20.1 133.6 %all-gather.5.cloned.1.call-start = ((), (), s32[]{:S(2)}) async-start(), calls=%async_computation.3 | async-start | bytes 16220160 | tf_op jit(solution)/shard_map/all_gather | solution.py:193
  20.1 7.6 %collective-permute-start = (bf16[120,256]{1,0:T(8,128)(2,1)S(1)}, bf16[120,256]{1,0:T(8,128)(2,1)S(1)}, u32[]{:S(2)}, u32[]{:S(2)}) collective-permute-start(bf16[120,256]{1,0:T(8,128)(2,1)S(1)} %get-tuple-element.53), channel_id=1, source_target_pairs={{0,8},{1,9},{2,10},{3,11},{4,12},{5,13},{6,14},{7,15},{8,16},{9,17... | collective-permute-start | bytes 184328 | tf_op jit(solution)/shard_map/ppermute | solution.py:70
  21.5 8.5 %collective-permute-start.1 = (bf16[120,256]{1,0:T(8,128)(2,1)S(1)}, bf16[120,256]{1,0:T(8,128)(2,1)S(1)}, u32[]{:S(2)}, u32[]{:S(2)}) collective-permute-start(bf16[120,256]{1,0:T(8,128)(2,1)S(1)} %get-tuple-element.53), channel_id=1, source_target_pairs={{0,16},{1,17},{2,18},{3,19},{4,20},{5,21},{6,22},{7,23},{8,24},{9,... | collective-permute-start | bytes 184328 | tf_op jit(solution)/shard_map/ppermute | solution.py:70
  24.1 6.5 %collective-permute-start.2 = (bf16[120,256]{1,0:T(8,128)(2,1)S(1)}, bf16[120,256]{1,0:T(8,128)(2,1)S(1)}, u32[]{:S(2)}, u32[]{:S(2)}) collective-permute-start(bf16[120,256]{1,0:T(8,128)(2,1)S(1)} %get-tuple-element.53), channel_id=1, source_target_pairs={{0,24},{1,25},{2,26},{3,27},{4,28},{5,29},{6,30},{7,31},{8,0},{9,1... | collective-permute-start | bytes 184328 | tf_op jit(solution)/shard_map/ppermute | solution.py:70
  26.5 8.9 %collective-permute-start.9 = (bf16[4,120,256]{2,1,0:T(8,128)(2,1)S(1)}, bf16[4,120,256]{2,1,0:T(8,128)(2,1)S(1)}, u32[]{:S(2)}, u32[]{:S(2)}) collective-permute-start(bf16[4,120,256]{2,1,0:T(8,128)(2,1)S(1)} %bitcast_dynamic-update-slice_fusion.20), channel_id=1, source_target_pairs={{0,8},{1,9},{2,10},{3,11},{4,12},{5,13},{6,14},{7,15},{8,16},{9,17... | collective-permute-start | bytes 737288 | tf_op jit(solution)/shard_map/ppermute | solution.py:70
  26.9 10.2 %collective-permute-start.10 = (bf16[4,120,256]{2,1,0:T(8,128)(2,1)S(1)}, bf16[4,120,256]{2,1,0:T(8,128)(2,1)S(1)}, u32[]{:S(2)}, u32[]{:S(2)}) collective-permute-start(bf16[4,120,256]{2,1,0:T(8,128)(2,1)S(1)} %bitcast_dynamic-update-slice_fusion.20), channel_id=1, source_target_pairs={{0,16},{1,17},{2,18},{3,19},{4,20},{5,21},{6,22},{7,23},{8,24},{9,... | collective-permute-start | bytes 737288 | tf_op jit(solution)/shard_map/ppermute | solution.py:70
  27.7 13.4 %collective-permute-start.11 = (bf16[4,120,256]{2,1,0:T(8,128)(2,1)S(1)}, bf16[4,120,256]{2,1,0:T(8,128)(2,1)S(1)}, u32[]{:S(2)}, u32[]{:S(2)}) collective-permute-start(bf16[4,120,256]{2,1,0:T(8,128)(2,1)S(1)} %bitcast_dynamic-update-slice_fusion.20), channel_id=1, source_target_pairs={{0,24},{1,25},{2,26},{3,27},{4,28},{5,29},{6,30},{7,31},{8,0},{9,1... | collective-permute-start | bytes 737288 | tf_op jit(solution)/shard_map/ppermute | solution.py:70
  31.2 9.9 %collective-permute-start.3 = (bf16[4,120,256]{2,1,0:T(8,128)(2,1)}, bf16[4,120,256]{2,1,0:T(8,128)(2,1)S(1)}, u32[]{:S(2)}, u32[]{:S(2)}) collective-permute-start(bf16[4,120,256]{2,1,0:T(8,128)(2,1)} %bitcast_dynamic-update-slice_fusion.24), channel_id=1, source_target_pairs={{0,2},{1,3},{2,4},{3,5},{4,6},{5,7},{6,0},{7,1},{8,10},{9,11},{10,... | collective-permute-start | bytes 737288 | tf_op jit(solution)/shard_map/ppermute | solution.py:70
  31.2 15.3 %collective-permute-start.4 = (bf16[4,120,256]{2,1,0:T(8,128)(2,1)}, bf16[4,120,256]{2,1,0:T(8,128)(2,1)S(1)}, u32[]{:S(2)}, u32[]{:S(2)}) collective-permute-start(bf16[4,120,256]{2,1,0:T(8,128)(2,1)} %bitcast_dynamic-update-slice_fusion.24), channel_id=1, source_target_pairs={{0,4},{1,5},{2,6},{3,7},{4,0},{5,1},{6,2},{7,3},{8,12},{9,13},{10,... | collective-permute-start | bytes 737288 | tf_op jit(solution)/shard_map/ppermute | solution.py:70
  35.5 11.1 %collective-permute-start.5 = (bf16[4,120,256]{2,1,0:T(8,128)(2,1)}, bf16[4,120,256]{2,1,0:T(8,128)(2,1)S(1)}, u32[]{:S(2)}, u32[]{:S(2)}) collective-permute-start(bf16[4,120,256]{2,1,0:T(8,128)(2,1)} %bitcast_dynamic-update-slice_fusion.24), channel_id=1, source_target_pairs={{0,6},{1,7},{2,0},{3,1},{4,2},{5,3},{6,4},{7,5},{8,14},{9,15},{10,... | collective-permute-start | bytes 737288 | tf_op jit(solution)/shard_map/ppermute | solution.py:70
  46.6 6.8 %collective-permute-start.13 = (bf16[4,4,120,256]{3,2,1,0:T(8,128)(2,1)S(1)}, bf16[4,4,120,256]{3,2,1,0:T(8,128)(2,1)}, u32[]{:S(2)}, u32[]{:S(2)}) collective-permute-start(bf16[4,4,120,256]{3,2,1,0:T(8,128)(2,1)S(1)} %bitcast_dynamic-update-slice_fusion.4), channel_id=1, source_target_pairs={{0,1},{1,0},{2,3},{3,2},{4,5},{5,4},{6,7},{7,6},{8,9},{9,8},{10,11... | collective-permute-start | bytes 2949128 | tf_op jit(solution)/shard_map/ppermute | solution.py:82
  58.9 5.9 %collective-permute-start.14 = (bf16[120,512]{1,0:T(8,128)(2,1)S(1)}, bf16[120,512]{1,0:T(8,128)(2,1)S(1)}, u32[]{:S(2)}, u32[]{:S(2)}) collective-permute-start(bf16[120,512]{1,0:T(8,128)(2,1)S(1)} %get-tuple-element.49), channel_id=1, source_target_pairs={{0,32},{32,64},{64,96},{96,0},{1,33},{33,65},{65,97},{97,1},{2,34}... | collective-permute-start | bytes 368648 | tf_op jit(solution)/shard_map/ppermute | solution.py:43
  60.2 8.2 %collective-permute-start.15 = (bf16[120,512]{1,0:T(8,128)(2,1)S(1)}, bf16[120,512]{1,0:T(8,128)(2,1)S(1)}, u32[]{:S(2)}, u32[]{:S(2)}) collective-permute-start(bf16[120,512]{1,0:T(8,128)(2,1)S(1)} %get-tuple-element.50), channel_id=1, source_target_pairs={{0,64},{32,96},{64,0},{96,32},{1,65},{33,97},{65,1},{97,33},{2,66}... | collective-permute-start | bytes 368648 | tf_op jit(solution)/shard_map/ppermute | solution.py:43
  69.6 7.3 %collective-permute-start.29 = (bf16[120,512]{1,0:T(8,128)(2,1)S(1)}, bf16[120,512]{1,0:T(8,128)(2,1)S(1)}, u32[]{:S(2)}, u32[]{:S(2)}) collective-permute-start(bf16[120,512]{1,0:T(8,128)(2,1)S(1)} %get-tuple-element.45), channel_id=1, source_target_pairs={{0,96},{32,0},{64,32},{96,64},{1,97},{33,1},{65,33},{97,65},{2,98}... | collective-permute-start | bytes 368648 | tf_op jit(solution)/shard_map/ppermute | solution.py:43
  79.7 16.8 %collective-permute-start.23 = (bf16[120,1024]{1,0:T(8,128)(2,1)S(1)}, bf16[120,1024]{1,0:T(8,128)(2,1)S(1)}, u32[]{:S(2)}, u32[]{:S(2)}) collective-permute-start(bf16[120,1024]{1,0:T(8,128)(2,1)S(1)} %pad_maximum_fusion.1), channel_id=1, source_target_pairs={{0,0},{4,1},{8,2},{12,3},{16,4},{20,5},{24,6},{28,7},{32,8},{36,9}... | collective-permute-start | bytes 737288 | tf_op jit(solution)/shard_map/ppermute | solution.py:200
  90.1 15.5 %collective-permute-start.17 = (bf16[120,512]{1,0:T(8,128)(2,1)S(1)}, bf16[120,512]{1,0:T(8,128)(2,1)S(1)}, u32[]{:S(2)}, u32[]{:S(2)}) collective-permute-start(bf16[120,512]{1,0:T(8,128)(2,1)S(1)} %get-tuple-element.46), channel_id=1, source_target_pairs={{0,32},{32,64},{64,96},{96,0},{1,33},{33,65},{65,97},{97,1},{2,34}... | collective-permute-start | bytes 368648 | tf_op jit(solution)/shard_map/ppermute | solution.py:43
  91.7 16.6 %collective-permute-start.18 = (bf16[120,512]{1,0:T(8,128)(2,1)S(1)}, bf16[120,512]{1,0:T(8,128)(2,1)S(1)}, u32[]{:S(2)}, u32[]{:S(2)}) collective-permute-start(bf16[120,512]{1,0:T(8,128)(2,1)S(1)} %get-tuple-element.48), channel_id=1, source_target_pairs={{0,64},{32,96},{64,0},{96,32},{1,65},{33,97},{65,1},{97,33},{2,66}... | collective-permute-start | bytes 368648 | tf_op jit(solution)/shard_map/ppermute | solution.py:43
  94.5 13.8 %collective-permute-start.19 = (bf16[120,512]{1,0:T(8,128)(2,1)S(1)}, bf16[120,512]{1,0:T(8,128)(2,1)S(1)}, u32[]{:S(2)}, u32[]{:S(2)}) collective-permute-start(bf16[120,512]{1,0:T(8,128)(2,1)S(1)} %get-tuple-element.47), channel_id=1, source_target_pairs={{0,96},{32,0},{64,32},{96,64},{1,97},{33,1},{65,33},{97,65},{2,98}... | collective-permute-start | bytes 368648 | tf_op jit(solution)/shard_map/ppermute | solution.py:43
  96.5 28.2 %collective-permute-start.24 = (bf16[120,1024]{1,0:T(8,128)(2,1)S(1)}, bf16[120,1024]{1,0:T(8,128)(2,1)S(1)}, u32[]{:S(2)}, u32[]{:S(2)}) collective-permute-start(bf16[120,1024]{1,0:T(8,128)(2,1)S(1)} %collective-permute-done.23), channel_id=1, source_target_pairs={{0,32},{32,64},{64,96},{96,0},{1,33},{33,65},{65,97},{97,1},{2,34}... | collective-permute-start | bytes 737288 | tf_op jit(solution)/shard_map/ppermute | solution.py:43
  96.6 28.9 %collective-permute-start.25 = (bf16[120,1024]{1,0:T(8,128)(2,1)S(1)}, bf16[120,1024]{1,0:T(8,128)(2,1)S(1)}, u32[]{:S(2)}, u32[]{:S(2)}) collective-permute-start(bf16[120,1024]{1,0:T(8,128)(2,1)S(1)} %collective-permute-done.23), channel_id=1, source_target_pairs={{0,64},{32,96},{64,0},{96,32},{1,65},{33,97},{65,1},{97,33},{2,66}... | collective-permute-start | bytes 737288 | tf_op jit(solution)/shard_map/ppermute | solution.py:43
  97.8 18.2 %all-to-all-start.1 = ((f32[128,2,128]{2,1,0:T(2,128)}), f32[128,2,128]{2,1,0:T(2,128)S(1)}, u32[]{:S(2)}, u32[]{:S(2)}) async-start(f32[128,2,128]{2,1,0:T(2,128)} %bitcast.38), calls=%async_computation.1 | async-start | bytes 262144 | tf_op jit(solution)/shard_map/all_to_all | solution.py:206
  105.7 20.5 %collective-permute-start.26 = (bf16[120,1024]{1,0:T(8,128)(2,1)S(1)}, bf16[120,1024]{1,0:T(8,128)(2,1)S(1)}, u32[]{:S(2)}, u32[]{:S(2)}) collective-permute-start(bf16[120,1024]{1,0:T(8,128)(2,1)S(1)} %collective-permute-done.23), channel_id=1, source_target_pairs={{0,96},{32,0},{64,32},{96,64},{1,97},{33,1},{65,33},{97,65},{2,98}... | collective-permute-start | bytes 737288 | tf_op jit(solution)/shard_map/ppermute | solution.py:43
  108.3 10.0 %collective-permute-start.22 = (bf16[120,512]{1,0:T(8,128)(2,1)S(1)}, bf16[120,512]{1,0:T(8,128)(2,1)S(1)}, u32[]{:S(2)}, u32[]{:S(2)}) collective-permute-start(bf16[120,512]{1,0:T(8,128)(2,1)S(1)} %fusion.26), channel_id=1, source_target_pairs={{0,96},{32,0},{64,32},{96,64},{1,97},{33,1},{65,33},{97,65},{2,98}... | collective-permute-start | bytes 368648 | tf_op jit(solution)/shard_map/ppermute | solution.py:43
  109.0 9.4 %collective-permute-start.21 = (bf16[120,512]{1,0:T(8,128)(2,1)S(1)}, bf16[120,512]{1,0:T(8,128)(2,1)S(1)}, u32[]{:S(2)}, u32[]{:S(2)}) collective-permute-start(bf16[120,512]{1,0:T(8,128)(2,1)S(1)} %fusion.26), channel_id=1, source_target_pairs={{0,64},{32,96},{64,0},{96,32},{1,65},{33,97},{65,1},{97,33},{2,66}... | collective-permute-start | bytes 368648 | tf_op jit(solution)/shard_map/ppermute | solution.py:43
  118.4 6.3 %collective-permute-start.20 = (bf16[120,512]{1,0:T(8,128)(2,1)S(1)}, bf16[120,512]{1,0:T(8,128)(2,1)S(1)}, u32[]{:S(2)}, u32[]{:S(2)}) collective-permute-start(bf16[120,512]{1,0:T(8,128)(2,1)S(1)} %fusion.26), channel_id=1, source_target_pairs={{0,32},{32,64},{64,96},{96,0},{1,33},{33,65},{65,97},{97,1},{2,34}... | collective-permute-start | bytes 368648 | tf_op jit(solution)/shard_map/ppermute | solution.py:43
  130.5 23.1 %all-to-all-start = ((bf16[32,16,384]{2,1,0:T(8,128)(2,1)}), bf16[32,16,384]{2,1,0:T(8,128)(2,1)S(1)}, u32[]{:S(2)}, u32[]{:S(2)}) async-start(bf16[32,16,384]{2,1,0:T(8,128)(2,1)} %pad_maximum_fusion), calls=%async_computation | async-start | bytes 786432 | tf_op jit(solution)/shard_map/all_to_all | solution.py:232
  153.7 19.7 %collective-permute-start.30 = (f32[16,384]{1,0:T(8,128)S(1)}, f32[16,384]{1,0:T(8,128)S(1)}, u32[]{:S(2)}, u32[]{:S(2)}) collective-permute-start(f32[16,384]{1,0:T(8,128)S(1)} %convert_reduce_fusion), channel_id=1, source_target_pairs={{0,32},{32,64},{64,96},{96,0},{1,33},{33,65},{65,97},{97,1},{2,34}... | collective-permute-start | bytes 73736 | tf_op jit(solution)/shard_map/ppermute | solution.py:43
  155.2 18.3 %collective-permute-start.31 = (f32[16,384]{1,0:T(8,128)S(1)}, f32[16,384]{1,0:T(8,128)S(1)}, u32[]{:S(2)}, u32[]{:S(2)}) collective-permute-start(f32[16,384]{1,0:T(8,128)S(1)} %convert_reduce_fusion), channel_id=1, source_target_pairs={{0,64},{32,96},{64,0},{96,32},{1,65},{33,97},{65,1},{97,33},{2,66}... | collective-permute-start | bytes 73736 | tf_op jit(solution)/shard_map/ppermute | solution.py:43
  157.3 16.2 %collective-permute-start.32 = (f32[16,384]{1,0:T(8,128)S(1)}, f32[16,384]{1,0:T(8,128)S(1)}, u32[]{:S(2)}, u32[]{:S(2)}) collective-permute-start(f32[16,384]{1,0:T(8,128)S(1)} %convert_reduce_fusion), channel_id=1, source_target_pairs={{0,96},{32,0},{64,32},{96,64},{1,97},{33,1},{65,33},{97,65},{2,98}... | collective-permute-start | bytes 73736 | tf_op jit(solution)/shard_map/ppermute | solution.py:43
  (15 other events, 145.1 us)
Sparse Core Ops, SparseCore 0:
  20.2 50.5 all-gather.2
  77.9 74.9 all-gather.4

commit v4 on v3

--- a/solution.py
+++ b/solution.py
@@ -173,7 +173,13 @@
     gram_rows = P_SIZE // col_count
     low = jnp.bfloat16
 
-    rest = (second_panel - precise(first_panel, second_lead)).astype(low)
+    share = jnp.dot(
+        first_panel,
+        second_lead,
+        precision=lax.Precision.HIGH,
+        preferred_element_type=jnp.float32,
+    )
+    rest = (second_panel - share).astype(low)
     left, right = spread_lines(rest)
     first_low = after(first_panel, left).astype(low)
     first_rows = lax.all_gather(first_low, "col", axis=0, tiled=True)

time: 182 us -> 182 us (level)
    dot_general x5 -> x4, matrix products: 5.47 us -> 3.7 us  [precise(): jnp.dot(left, right, precision=lax.Precision.HIGHEST, preferred_element_t...]
where the time goes in v4:
time: 182 us; the launch traced here: 181 us
  starting transfers between devices  69.2 us (38%)
  waiting for transfers between devices  41.8 us (23%)
  matrix products  15.8 us (9%)
  between operations  15.4 us (8%)
  Pallas kernels  14.8 us (8%)
  local copies, waits for them, and re-layouts  12.4 us (7%)
  other arithmetic  11.4 us (6%)
    ppermute x18, starting transfers between devices, shift_rows(): lax.ppermute(value, 'row', [(i, (i + step) % size) for i in range(size)])  24.5 us
    ppermute x12, starting transfers between devices, shift_chips(): return lax.ppermute(value, 'col', perm)  19.1 us
    ppermute x18, waiting for transfers between devices, shift_rows(): lax.ppermute(value, 'row', [(i, (i + step) % size) for i in range(size)])  16.3 us
    pallas_call x1, Pallas kernels, build_tiles(): pl.pallas_call(tile_kernel, grid_spec=pltpu.PrefetchScalarGridSpec(num_sc...  14.8 us
    dot_general x5, matrix products, contract_rows(): lax.dot_general(left, right, (((0,), (0,)), ((), ())), preferred_element_...  10.7 us
    all_to_all x1, waiting for transfers between devices, shards(): sums = lax.all_to_all(sums, 'col', split_axis=0, concat_axis=0, tiled=True)  9.05 us
    all_to_all x1, starting transfers between devices, shards(): sums = lax.all_to_all(sums, 'col', split_axis=0, concat_axis=0, tiled=True)  9.02 us
    all_to_all x1, starting transfers between devices, shards(): lax.all_to_all(lists, ('row', 'col'), split_axis=0, concat_axis=0, tiled=...  7.15 us
  transfers between devices with their start and end apart: 37, of which 13 were waited for; matrix products, arithmetic and copies ran while one was open for 19% of the time, Pallas kernels for 8%

profile of v4, /device:TPU:1, one launch (start us, length us, event | category | flops | bytes accessed | tf_op | source)
XLA Modules:
  0.0 180.9 jit_solution(6977707961130495612)
XLA Ops:
  8.4 1.5 fusion.3
  9.9 2.5 %collective-permute-start.6 = (bf16[120,256]{1,0:T(8,128)(2,1)S(1)}, bf16[120,256]{1,0:T(8,128)(2,1)S(1)}, u32[]{:S(2)}, u32[]{:S(2)}) collective-permute-start(bf16[120,256]{1,0:T(8,128)(2,1)S(1)} %get-tuple-element.52), channel_id=1, source_target_pairs={{0,2},{1,3},{2,4},{3,5},{4,6},{5,7},{6,0},{7,1},{8,10},{9,11},{10,... | collective-permute-start | bytes 184328 | tf_op jit(solution)/shard_map/ppermute | solution.py:70
  12.4 3.3 %collective-permute-start.7 = (bf16[120,256]{1,0:T(8,128)(2,1)S(1)}, bf16[120,256]{1,0:T(8,128)(2,1)S(1)}, u32[]{:S(2)}, u32[]{:S(2)}) collective-permute-start(bf16[120,256]{1,0:T(8,128)(2,1)S(1)} %get-tuple-element.52), channel_id=1, source_target_pairs={{0,4},{1,5},{2,6},{3,7},{4,0},{5,1},{6,2},{7,3},{8,12},{9,13},{10,... | collective-permute-start | bytes 184328 | tf_op jit(solution)/shard_map/ppermute | solution.py:70
  16.6 1.6 collective-permute-done.7
  21.2 2.6 %collective-permute-start.1 = (bf16[120,256]{1,0:T(8,128)(2,1)S(1)}, bf16[120,256]{1,0:T(8,128)(2,1)S(1)}, u32[]{:S(2)}, u32[]{:S(2)}) collective-permute-start(bf16[120,256]{1,0:T(8,128)(2,1)S(1)} %get-tuple-element.53), channel_id=1, source_target_pairs={{0,16},{1,17},{2,18},{3,19},{4,20},{5,21},{6,22},{7,23},{8,24},{9,... | collective-permute-start | bytes 184328 | tf_op jit(solution)/shard_map/ppermute | solution.py:70
  27.4 1.6 collective-permute-start.11
  30.9 3.1 %collective-permute-start.4 = (bf16[4,120,256]{2,1,0:T(8,128)(2,1)}, bf16[4,120,256]{2,1,0:T(8,128)(2,1)S(1)}, u32[]{:S(2)}, u32[]{:S(2)}) collective-permute-start(bf16[4,120,256]{2,1,0:T(8,128)(2,1)} %bitcast_dynamic-update-slice_fusion.24), channel_id=1, source_target_pairs={{0,4},{1,5},{2,6},{3,7},{4,0},{5,1},{6,2},{7,3},{8,12},{9,13},{10,... | collective-permute-start | bytes 737288 | tf_op jit(solution)/shard_map/ppermute | solution.py:70
  35.2 1.6 collective-permute-start.5
  36.9 4.0 %collective-permute-done.11 = bf16[4,120,256]{2,1,0:T(8,128)(2,1)S(1)} collective-permute-done((bf16[4,120,256]{2,1,0:T(8,128)(2,1)S(1)}, bf16[4,120,256]{2,1,0:T(8,128)(2,1)S(1)}, u32[]{:S(2)}, u32[]{:S(2)}) %collective-permute-start.11) | collective-permute-done | bytes 245792 | tf_op jit(solution)/shard_map/ppermute | solution.py:70
  40.9 5.3 %convert_element_type.75 = bf16[3840,480]{0,1:T(8,128)(2,1)} convert(f32[3840,480]{0,1:T(8,128)} %param.10) | non-fusion elementwise | flops 1843200 | bytes 11059200 | tf_op jit(solution)/shard_map/convert_element_type | solution.py:188
  46.3 4.5 %collective-permute-start.13 = (bf16[4,4,120,256]{3,2,1,0:T(8,128)(2,1)S(1)}, bf16[4,4,120,256]{3,2,1,0:T(8,128)(2,1)}, u32[]{:S(2)}, u32[]{:S(2)}) collective-permute-start(bf16[4,4,120,256]{3,2,1,0:T(8,128)(2,1)S(1)} %bitcast_dynamic-update-slice_fusion.4), channel_id=1, source_target_pairs={{0,1},{1,0},{2,3},{3,2},{4,5},{5,4},{6,7},{7,6},{8,9},{9,8},{10,11... | collective-permute-start | bytes 2949128 | tf_op jit(solution)/shard_map/ppermute | solution.py:82
  51.4 1.7 collective-permute-done.13
  54.5 1.7 bitcast_dynamic-update-slice_fusion
  59.9 2.5 %collective-permute-start.15 = (bf16[120,512]{1,0:T(8,128)(2,1)S(1)}, bf16[120,512]{1,0:T(8,128)(2,1)S(1)}, u32[]{:S(2)}, u32[]{:S(2)}) collective-permute-start(bf16[120,512]{1,0:T(8,128)(2,1)S(1)} %get-tuple-element.50), channel_id=1, source_target_pairs={{0,64},{32,96},{64,0},{96,32},{1,65},{33,97},{65,1},{97,33},{2,66}... | collective-permute-start | bytes 368648 | tf_op jit(solution)/shard_map/ppermute | solution.py:43
  64.5 3.5 %collective-permute-done.15 = bf16[120,512]{1,0:T(8,128)(2,1)S(1)} collective-permute-done((bf16[120,512]{1,0:T(8,128)(2,1)S(1)}, bf16[120,512]{1,0:T(8,128)(2,1)S(1)}, u32[]{:S(2)}, u32[]{:S(2)}) %collective-permute-start.15) | collective-permute-done | bytes 122912 | tf_op jit(solution)/shard_map/ppermute | solution.py:43
  69.3 1.6 collective-permute-start.29
  73.2 3.4 %collective-permute-done.28 = bf16[120,512]{1,0:T(8,128)(2,1)S(1)} collective-permute-done((bf16[120,512]{1,0:T(8,128)(2,1)S(1)}, bf16[120,512]{1,0:T(8,128)(2,1)S(1)}, u32[]{:S(2)}, u32[]{:S(2)}) %collective-permute-start.28) | collective-permute-done | bytes 122912 | tf_op jit(solution)/shard_map/ppermute | solution.py:43
  79.4 4.7 %collective-permute-start.23 = (bf16[120,1024]{1,0:T(8,128)(2,1)S(1)}, bf16[120,1024]{1,0:T(8,128)(2,1)S(1)}, u32[]{:S(2)}, u32[]{:S(2)}) collective-permute-start(bf16[120,1024]{1,0:T(8,128)(2,1)S(1)} %pad_maximum_fusion.1), channel_id=1, source_target_pairs={{0,0},{4,1},{8,2},{12,3},{16,4},{20,5},{24,6},{28,7},{32,8},{36,9}... | collective-permute-start | bytes 737288 | tf_op jit(solution)/shard_map/ppermute | solution.py:206
  84.2 5.6 %fusion = bf16[480,512]{1,0:T(8,128)(2,1)S(1)} fusion(bf16[3840,480]{0,1:T(8,128)(2,1)} %convert_element_type.75, bf16[3840,512]{1,0:T(8,128)(2,1)} %all-gather.3.cloned.1.call-done), kind=kOutput, calls=%fused_computation.1 | convolution fusion | flops 1887928320 | bytes 8110080 | tf_op jit(solution)/shard_map/dot_general | solution.py:22
  89.9 1.6 collective-permute-start.17
  91.4 2.8 %collective-permute-start.18 = (bf16[120,512]{1,0:T(8,128)(2,1)S(1)}, bf16[120,512]{1,0:T(8,128)(2,1)S(1)}, u32[]{:S(2)}, u32[]{:S(2)}) collective-permute-start(bf16[120,512]{1,0:T(8,128)(2,1)S(1)} %get-tuple-element.48), channel_id=1, source_target_pairs={{0,64},{32,96},{64,0},{96,32},{1,65},{33,97},{65,1},{97,33},{2,66}... | collective-permute-start | bytes 368648 | tf_op jit(solution)/shard_map/ppermute | solution.py:43
  94.2 2.0 %collective-permute-start.19 = (bf16[120,512]{1,0:T(8,128)(2,1)S(1)}, bf16[120,512]{1,0:T(8,128)(2,1)S(1)}, u32[]{:S(2)}, u32[]{:S(2)}) collective-permute-start(bf16[120,512]{1,0:T(8,128)(2,1)S(1)} %get-tuple-element.47), channel_id=1, source_target_pairs={{0,96},{32,0},{64,32},{96,64},{1,97},{33,1},{65,33},{97,65},{2,98}... | collective-permute-start | bytes 368648 | tf_op jit(solution)/shard_map/ppermute | solution.py:43
  97.5 7.2 %all-to-all-start.1 = ((f32[128,2,128]{2,1,0:T(2,128)}), f32[128,2,128]{2,1,0:T(2,128)S(1)}, u32[]{:S(2)}, u32[]{:S(2)}) async-start(f32[128,2,128]{2,1,0:T(2,128)} %bitcast.38), calls=%async_computation.1 | async-start | bytes 262144 | tf_op jit(solution)/shard_map/all_to_all | solution.py:212
  105.4 2.6 %collective-permute-start.26 = (bf16[120,1024]{1,0:T(8,128)(2,1)S(1)}, bf16[120,1024]{1,0:T(8,128)(2,1)S(1)}, u32[]{:S(2)}, u32[]{:S(2)}) collective-permute-start(bf16[120,1024]{1,0:T(8,128)(2,1)S(1)} %collective-permute-done.23), channel_id=1, source_target_pairs={{0,96},{32,0},{64,32},{96,64},{1,97},{33,1},{65,33},{97,65},{2,98}... | collective-permute-start | bytes 737288 | tf_op jit(solution)/shard_map/ppermute | solution.py:43
  108.8 6.9 %all-to-all-done.1 = f32[128,2,128]{2,1,0:T(2,128)S(1)} async-done(((f32[128,2,128]{2,1,0:T(2,128)}), f32[128,2,128]{2,1,0:T(2,128)S(1)}, u32[]{:S(2)}, u32[]{:S(2)}) %all-to-all-start.1) | async-done | bytes 131104 | tf_op jit(solution)/shard_map/all_to_all | solution.py:212
  118.1 6.3 %collective-permute-done.20 = bf16[120,512]{1,0:T(8,128)(2,1)S(1)} collective-permute-done((bf16[120,512]{1,0:T(8,128)(2,1)S(1)}, bf16[120,512]{1,0:T(8,128)(2,1)S(1)}, u32[]{:S(2)}, u32[]{:S(2)}) %collective-permute-start.20) | collective-permute-done | bytes 122912 | tf_op jit(solution)/shard_map/ppermute | solution.py:43
  128.0 1.4 convolution_convert_fusion
  130.2 9.0 %all-to-all-start = ((bf16[32,16,384]{2,1,0:T(8,128)(2,1)}), bf16[32,16,384]{2,1,0:T(8,128)(2,1)S(1)}, u32[]{:S(2)}, u32[]{:S(2)}) async-start(bf16[32,16,384]{2,1,0:T(8,128)(2,1)} %pad_maximum_fusion), calls=%async_computation | async-start | bytes 786432 | tf_op jit(solution)/shard_map/all_to_all | solution.py:238
  144.3 9.1 %all-to-all-done = bf16[32,16,384]{2,1,0:T(8,128)(2,1)S(1)} async-done(((bf16[32,16,384]{2,1,0:T(8,128)(2,1)}), bf16[32,16,384]{2,1,0:T(8,128)(2,1)S(1)}, u32[]{:S(2)}, u32[]{:S(2)}) %all-to-all-start) | async-done | bytes 393248 | tf_op jit(solution)/shard_map/all_to_all | solution.py:238
  153.4 1.5 collective-permute-start.30
  154.9 2.1 %collective-permute-start.31 = (f32[16,384]{1,0:T(8,128)S(1)}, f32[16,384]{1,0:T(8,128)S(1)}, u32[]{:S(2)}, u32[]{:S(2)}) collective-permute-start(f32[16,384]{1,0:T(8,128)S(1)} %convert_reduce_fusion), channel_id=1, source_target_pairs={{0,64},{32,96},{64,0},{96,32},{1,65},{33,97},{65,1},{97,33},{2,66}... | collective-permute-start | bytes 73736 | tf_op jit(solution)/shard_map/ppermute | solution.py:43
  158.3 14.8 %shard_map.145 = bf16[4,32,2,128,128]{4,3,2,1,0:T(8,128)(2,1)} custom-call(s32[32,8]{1,0:T(8,128)} %add_select_fusion.1.blocks_ref, s32[32,8,128]{2,1,0:T(8,128)} %fusion.32.index_ref, bf16[32,480,512]{2,1,0:T(8,128)(2,1)} %all-gather.5.cloned.1.call-done.band_ref), custom_call_target="tpu_custom_call" | custom-call | flops 4026531840 | bytes 25000000 | tf_op jit(solution)/shard_map/pallas_call | solution.py:111
  (150 shorter events, 42.0 us)
Async XLA Ops:
  7.2 77.0 %all-gather.3.cloned.1.call-start = ((), (), s32[]{:S(2)}) async-start(), calls=%async_computation.2 | async-start | bytes 4055040 | tf_op jit(solution)/shard_map/all_gather | solution.py:185
  9.9 6.7 %collective-permute-start.6 = (bf16[120,256]{1,0:T(8,128)(2,1)S(1)}, bf16[120,256]{1,0:T(8,128)(2,1)S(1)}, u32[]{:S(2)}, u32[]{:S(2)}) collective-permute-start(bf16[120,256]{1,0:T(8,128)(2,1)S(1)} %get-tuple-element.52), channel_id=1, source_target_pairs={{0,2},{1,3},{2,4},{3,5},{4,6},{5,7},{6,0},{7,1},{8,10},{9,11},{10,... | collective-permute-start | bytes 184328 | tf_op jit(solution)/shard_map/ppermute | solution.py:70
  12.4 5.7 %collective-permute-start.7 = (bf16[120,256]{1,0:T(8,128)(2,1)S(1)}, bf16[120,256]{1,0:T(8,128)(2,1)S(1)}, u32[]{:S(2)}, u32[]{:S(2)}) collective-permute-start(bf16[120,256]{1,0:T(8,128)(2,1)S(1)} %get-tuple-element.52), channel_id=1, source_target_pairs={{0,4},{1,5},{2,6},{3,7},{4,0},{5,1},{6,2},{7,3},{8,12},{9,13},{10,... | collective-permute-start | bytes 184328 | tf_op jit(solution)/shard_map/ppermute | solution.py:70
  19.8 133.6 %all-gather.5.cloned.1.call-start = ((), (), s32[]{:S(2)}) async-start(), calls=%async_computation.3 | async-start | bytes 16220160 | tf_op jit(solution)/shard_map/all_gather | solution.py:199
  19.9 7.6 %collective-permute-start = (bf16[120,256]{1,0:T(8,128)(2,1)S(1)}, bf16[120,256]{1,0:T(8,128)(2,1)S(1)}, u32[]{:S(2)}, u32[]{:S(2)}) collective-permute-start(bf16[120,256]{1,0:T(8,128)(2,1)S(1)} %get-tuple-element.53), channel_id=1, source_target_pairs={{0,8},{1,9},{2,10},{3,11},{4,12},{5,13},{6,14},{7,15},{8,16},{9,17... | collective-permute-start | bytes 184328 | tf_op jit(solution)/shard_map/ppermute | solution.py:70
  21.2 8.5 %collective-permute-start.1 = (bf16[120,256]{1,0:T(8,128)(2,1)S(1)}, bf16[120,256]{1,0:T(8,128)(2,1)S(1)}, u32[]{:S(2)}, u32[]{:S(2)}) collective-permute-start(bf16[120,256]{1,0:T(8,128)(2,1)S(1)} %get-tuple-element.53), channel_id=1, source_target_pairs={{0,16},{1,17},{2,18},{3,19},{4,20},{5,21},{6,22},{7,23},{8,24},{9,... | collective-permute-start | bytes 184328 | tf_op jit(solution)/shard_map/ppermute | solution.py:70
  23.8 6.5 %collective-permute-start.2 = (bf16[120,256]{1,0:T(8,128)(2,1)S(1)}, bf16[120,256]{1,0:T(8,128)(2,1)S(1)}, u32[]{:S(2)}, u32[]{:S(2)}) collective-permute-start(bf16[120,256]{1,0:T(8,128)(2,1)S(1)} %get-tuple-element.53), channel_id=1, source_target_pairs={{0,24},{1,25},{2,26},{3,27},{4,28},{5,29},{6,30},{7,31},{8,0},{9,1... | collective-permute-start | bytes 184328 | tf_op jit(solution)/shard_map/ppermute | solution.py:70
  26.2 8.9 %collective-permute-start.9 = (bf16[4,120,256]{2,1,0:T(8,128)(2,1)S(1)}, bf16[4,120,256]{2,1,0:T(8,128)(2,1)S(1)}, u32[]{:S(2)}, u32[]{:S(2)}) collective-permute-start(bf16[4,120,256]{2,1,0:T(8,128)(2,1)S(1)} %bitcast_dynamic-update-slice_fusion.20), channel_id=1, source_target_pairs={{0,8},{1,9},{2,10},{3,11},{4,12},{5,13},{6,14},{7,15},{8,16},{9,17... | collective-permute-start | bytes 737288 | tf_op jit(solution)/shard_map/ppermute | solution.py:70
  26.6 10.2 %collective-permute-start.10 = (bf16[4,120,256]{2,1,0:T(8,128)(2,1)S(1)}, bf16[4,120,256]{2,1,0:T(8,128)(2,1)S(1)}, u32[]{:S(2)}, u32[]{:S(2)}) collective-permute-start(bf16[4,120,256]{2,1,0:T(8,128)(2,1)S(1)} %bitcast_dynamic-update-slice_fusion.20), channel_id=1, source_target_pairs={{0,16},{1,17},{2,18},{3,19},{4,20},{5,21},{6,22},{7,23},{8,24},{9,... | collective-permute-start | bytes 737288 | tf_op jit(solution)/shard_map/ppermute | solution.py:70
  27.4 13.4 %collective-permute-start.11 = (bf16[4,120,256]{2,1,0:T(8,128)(2,1)S(1)}, bf16[4,120,256]{2,1,0:T(8,128)(2,1)S(1)}, u32[]{:S(2)}, u32[]{:S(2)}) collective-permute-start(bf16[4,120,256]{2,1,0:T(8,128)(2,1)S(1)} %bitcast_dynamic-update-slice_fusion.20), channel_id=1, source_target_pairs={{0,24},{1,25},{2,26},{3,27},{4,28},{5,29},{6,30},{7,31},{8,0},{9,1... | collective-permute-start | bytes 737288 | tf_op jit(solution)/shard_map/ppermute | solution.py:70
  30.9 9.9 %collective-permute-start.3 = (bf16[4,120,256]{2,1,0:T(8,128)(2,1)}, bf16[4,120,256]{2,1,0:T(8,128)(2,1)S(1)}, u32[]{:S(2)}, u32[]{:S(2)}) collective-permute-start(bf16[4,120,256]{2,1,0:T(8,128)(2,1)} %bitcast_dynamic-update-slice_fusion.24), channel_id=1, source_target_pairs={{0,2},{1,3},{2,4},{3,5},{4,6},{5,7},{6,0},{7,1},{8,10},{9,11},{10,... | collective-permute-start | bytes 737288 | tf_op jit(solution)/shard_map/ppermute | solution.py:70
  30.9 15.3 %collective-permute-start.4 = (bf16[4,120,256]{2,1,0:T(8,128)(2,1)}, bf16[4,120,256]{2,1,0:T(8,128)(2,1)S(1)}, u32[]{:S(2)}, u32[]{:S(2)}) collective-permute-start(bf16[4,120,256]{2,1,0:T(8,128)(2,1)} %bitcast_dynamic-update-slice_fusion.24), channel_id=1, source_target_pairs={{0,4},{1,5},{2,6},{3,7},{4,0},{5,1},{6,2},{7,3},{8,12},{9,13},{10,... | collective-permute-start | bytes 737288 | tf_op jit(solution)/shard_map/ppermute | solution.py:70
  35.2 11.1 %collective-permute-start.5 = (bf16[4,120,256]{2,1,0:T(8,128)(2,1)}, bf16[4,120,256]{2,1,0:T(8,128)(2,1)S(1)}, u32[]{:S(2)}, u32[]{:S(2)}) collective-permute-start(bf16[4,120,256]{2,1,0:T(8,128)(2,1)} %bitcast_dynamic-update-slice_fusion.24), channel_id=1, source_target_pairs={{0,6},{1,7},{2,0},{3,1},{4,2},{5,3},{6,4},{7,5},{8,14},{9,15},{10,... | collective-permute-start | bytes 737288 | tf_op jit(solution)/shard_map/ppermute | solution.py:70
  46.3 6.8 %collective-permute-start.13 = (bf16[4,4,120,256]{3,2,1,0:T(8,128)(2,1)S(1)}, bf16[4,4,120,256]{3,2,1,0:T(8,128)(2,1)}, u32[]{:S(2)}, u32[]{:S(2)}) collective-permute-start(bf16[4,4,120,256]{3,2,1,0:T(8,128)(2,1)S(1)} %bitcast_dynamic-update-slice_fusion.4), channel_id=1, source_target_pairs={{0,1},{1,0},{2,3},{3,2},{4,5},{5,4},{6,7},{7,6},{8,9},{9,8},{10,11... | collective-permute-start | bytes 2949128 | tf_op jit(solution)/shard_map/ppermute | solution.py:82
  58.6 5.9 %collective-permute-start.14 = (bf16[120,512]{1,0:T(8,128)(2,1)S(1)}, bf16[120,512]{1,0:T(8,128)(2,1)S(1)}, u32[]{:S(2)}, u32[]{:S(2)}) collective-permute-start(bf16[120,512]{1,0:T(8,128)(2,1)S(1)} %get-tuple-element.49), channel_id=1, source_target_pairs={{0,32},{32,64},{64,96},{96,0},{1,33},{33,65},{65,97},{97,1},{2,34}... | collective-permute-start | bytes 368648 | tf_op jit(solution)/shard_map/ppermute | solution.py:43
  59.9 8.2 %collective-permute-start.15 = (bf16[120,512]{1,0:T(8,128)(2,1)S(1)}, bf16[120,512]{1,0:T(8,128)(2,1)S(1)}, u32[]{:S(2)}, u32[]{:S(2)}) collective-permute-start(bf16[120,512]{1,0:T(8,128)(2,1)S(1)} %get-tuple-element.50), channel_id=1, source_target_pairs={{0,64},{32,96},{64,0},{96,32},{1,65},{33,97},{65,1},{97,33},{2,66}... | collective-permute-start | bytes 368648 | tf_op jit(solution)/shard_map/ppermute | solution.py:43
  69.3 7.3 %collective-permute-start.29 = (bf16[120,512]{1,0:T(8,128)(2,1)S(1)}, bf16[120,512]{1,0:T(8,128)(2,1)S(1)}, u32[]{:S(2)}, u32[]{:S(2)}) collective-permute-start(bf16[120,512]{1,0:T(8,128)(2,1)S(1)} %get-tuple-element.45), channel_id=1, source_target_pairs={{0,96},{32,0},{64,32},{96,64},{1,97},{33,1},{65,33},{97,65},{2,98}... | collective-permute-start | bytes 368648 | tf_op jit(solution)/shard_map/ppermute | solution.py:43
  79.4 16.8 %collective-permute-start.23 = (bf16[120,1024]{1,0:T(8,128)(2,1)S(1)}, bf16[120,1024]{1,0:T(8,128)(2,1)S(1)}, u32[]{:S(2)}, u32[]{:S(2)}) collective-permute-start(bf16[120,1024]{1,0:T(8,128)(2,1)S(1)} %pad_maximum_fusion.1), channel_id=1, source_target_pairs={{0,0},{4,1},{8,2},{12,3},{16,4},{20,5},{24,6},{28,7},{32,8},{36,9}... | collective-permute-start | bytes 737288 | tf_op jit(solution)/shard_map/ppermute | solution.py:206
  89.9 15.5 %collective-permute-start.17 = (bf16[120,512]{1,0:T(8,128)(2,1)S(1)}, bf16[120,512]{1,0:T(8,128)(2,1)S(1)}, u32[]{:S(2)}, u32[]{:S(2)}) collective-permute-start(bf16[120,512]{1,0:T(8,128)(2,1)S(1)} %get-tuple-element.46), channel_id=1, source_target_pairs={{0,32},{32,64},{64,96},{96,0},{1,33},{33,65},{65,97},{97,1},{2,34}... | collective-permute-start | bytes 368648 | tf_op jit(solution)/shard_map/ppermute | solution.py:43
  91.4 16.5 %collective-permute-start.18 = (bf16[120,512]{1,0:T(8,128)(2,1)S(1)}, bf16[120,512]{1,0:T(8,128)(2,1)S(1)}, u32[]{:S(2)}, u32[]{:S(2)}) collective-permute-start(bf16[120,512]{1,0:T(8,128)(2,1)S(1)} %get-tuple-element.48), channel_id=1, source_target_pairs={{0,64},{32,96},{64,0},{96,32},{1,65},{33,97},{65,1},{97,33},{2,66}... | collective-permute-start | bytes 368648 | tf_op jit(solution)/shard_map/ppermute | solution.py:43
  94.2 13.7 %collective-permute-start.19 = (bf16[120,512]{1,0:T(8,128)(2,1)S(1)}, bf16[120,512]{1,0:T(8,128)(2,1)S(1)}, u32[]{:S(2)}, u32[]{:S(2)}) collective-permute-start(bf16[120,512]{1,0:T(8,128)(2,1)S(1)} %get-tuple-element.47), channel_id=1, source_target_pairs={{0,96},{32,0},{64,32},{96,64},{1,97},{33,1},{65,33},{97,65},{2,98}... | collective-permute-start | bytes 368648 | tf_op jit(solution)/shard_map/ppermute | solution.py:43
  96.2 28.2 %collective-permute-start.24 = (bf16[120,1024]{1,0:T(8,128)(2,1)S(1)}, bf16[120,1024]{1,0:T(8,128)(2,1)S(1)}, u32[]{:S(2)}, u32[]{:S(2)}) collective-permute-start(bf16[120,1024]{1,0:T(8,128)(2,1)S(1)} %collective-permute-done.23), channel_id=1, source_target_pairs={{0,32},{32,64},{64,96},{96,0},{1,33},{33,65},{65,97},{97,1},{2,34}... | collective-permute-start | bytes 737288 | tf_op jit(solution)/shard_map/ppermute | solution.py:43
  96.3 28.8 %collective-permute-start.25 = (bf16[120,1024]{1,0:T(8,128)(2,1)S(1)}, bf16[120,1024]{1,0:T(8,128)(2,1)S(1)}, u32[]{:S(2)}, u32[]{:S(2)}) collective-permute-start(bf16[120,1024]{1,0:T(8,128)(2,1)S(1)} %collective-permute-done.23), channel_id=1, source_target_pairs={{0,64},{32,96},{64,0},{96,32},{1,65},{33,97},{65,1},{97,33},{2,66}... | collective-permute-start | bytes 737288 | tf_op jit(solution)/shard_map/ppermute | solution.py:43
  97.5 18.2 %all-to-all-start.1 = ((f32[128,2,128]{2,1,0:T(2,128)}), f32[128,2,128]{2,1,0:T(2,128)S(1)}, u32[]{:S(2)}, u32[]{:S(2)}) async-start(f32[128,2,128]{2,1,0:T(2,128)} %bitcast.38), calls=%async_computation.1 | async-start | bytes 262144 | tf_op jit(solution)/shard_map/all_to_all | solution.py:212
  105.4 20.5 %collective-permute-start.26 = (bf16[120,1024]{1,0:T(8,128)(2,1)S(1)}, bf16[120,1024]{1,0:T(8,128)(2,1)S(1)}, u32[]{:S(2)}, u32[]{:S(2)}) collective-permute-start(bf16[120,1024]{1,0:T(8,128)(2,1)S(1)} %collective-permute-done.23), channel_id=1, source_target_pairs={{0,96},{32,0},{64,32},{96,64},{1,97},{33,1},{65,33},{97,65},{2,98}... | collective-permute-start | bytes 737288 | tf_op jit(solution)/shard_map/ppermute | solution.py:43
  108.0 10.0 %collective-permute-start.22 = (bf16[120,512]{1,0:T(8,128)(2,1)S(1)}, bf16[120,512]{1,0:T(8,128)(2,1)S(1)}, u32[]{:S(2)}, u32[]{:S(2)}) collective-permute-start(bf16[120,512]{1,0:T(8,128)(2,1)S(1)} %fusion.26), channel_id=1, source_target_pairs={{0,96},{32,0},{64,32},{96,64},{1,97},{33,1},{65,33},{97,65},{2,98}... | collective-permute-start | bytes 368648 | tf_op jit(solution)/shard_map/ppermute | solution.py:43
  108.7 9.4 %collective-permute-start.21 = (bf16[120,512]{1,0:T(8,128)(2,1)S(1)}, bf16[120,512]{1,0:T(8,128)(2,1)S(1)}, u32[]{:S(2)}, u32[]{:S(2)}) collective-permute-start(bf16[120,512]{1,0:T(8,128)(2,1)S(1)} %fusion.26), channel_id=1, source_target_pairs={{0,64},{32,96},{64,0},{96,32},{1,65},{33,97},{65,1},{97,33},{2,66}... | collective-permute-start | bytes 368648 | tf_op jit(solution)/shard_map/ppermute | solution.py:43
  118.1 6.3 %collective-permute-start.20 = (bf16[120,512]{1,0:T(8,128)(2,1)S(1)}, bf16[120,512]{1,0:T(8,128)(2,1)S(1)}, u32[]{:S(2)}, u32[]{:S(2)}) collective-permute-start(bf16[120,512]{1,0:T(8,128)(2,1)S(1)} %fusion.26), channel_id=1, source_target_pairs={{0,32},{32,64},{64,96},{96,0},{1,33},{33,65},{65,97},{97,1},{2,34}... | collective-permute-start | bytes 368648 | tf_op jit(solution)/shard_map/ppermute | solution.py:43
  130.2 23.1 %all-to-all-start = ((bf16[32,16,384]{2,1,0:T(8,128)(2,1)}), bf16[32,16,384]{2,1,0:T(8,128)(2,1)S(1)}, u32[]{:S(2)}, u32[]{:S(2)}) async-start(bf16[32,16,384]{2,1,0:T(8,128)(2,1)} %pad_maximum_fusion), calls=%async_computation | async-start | bytes 786432 | tf_op jit(solution)/shard_map/all_to_all | solution.py:238
  153.4 19.7 %collective-permute-start.30 = (f32[16,384]{1,0:T(8,128)S(1)}, f32[16,384]{1,0:T(8,128)S(1)}, u32[]{:S(2)}, u32[]{:S(2)}) collective-permute-start(f32[16,384]{1,0:T(8,128)S(1)} %convert_reduce_fusion), channel_id=1, source_target_pairs={{0,32},{32,64},{64,96},{96,0},{1,33},{33,65},{65,97},{97,1},{2,34}... | collective-permute-start | bytes 73736 | tf_op jit(solution)/shard_map/ppermute | solution.py:43
  154.9 18.3 %collective-permute-start.31 = (f32[16,384]{1,0:T(8,128)S(1)}, f32[16,384]{1,0:T(8,128)S(1)}, u32[]{:S(2)}, u32[]{:S(2)}) collective-permute-start(f32[16,384]{1,0:T(8,128)S(1)} %convert_reduce_fusion), channel_id=1, source_target_pairs={{0,64},{32,96},{64,0},{96,32},{1,65},{33,97},{65,1},{97,33},{2,66}... | collective-permute-start | bytes 73736 | tf_op jit(solution)/shard_map/ppermute | solution.py:43
  157.0 16.2 %collective-permute-start.32 = (f32[16,384]{1,0:T(8,128)S(1)}, f32[16,384]{1,0:T(8,128)S(1)}, u32[]{:S(2)}, u32[]{:S(2)}) collective-permute-start(f32[16,384]{1,0:T(8,128)S(1)} %convert_reduce_fusion), channel_id=1, source_target_pairs={{0,96},{32,0},{64,32},{96,64},{1,97},{33,1},{65,33},{97,65},{2,98}... | collective-permute-start | bytes 73736 | tf_op jit(solution)/shard_map/ppermute | solution.py:43
  (15 other events, 144.8 us)
Sparse Core Ops, SparseCore 0:
  19.9 50.5 all-gather.2
  77.6 74.9 all-gather.4
